TPU v7x, 128 devices: a whole 4x4x4 slice. The times are simulated.
128 devices in a mesh: wa: 32 (over x, y, core), vert: 4 (over z).
Axes of the slice: x: 4, y: 4, z: 4, core: 2. Of those that a mesh axis runs over, the one named last changes fastest.
Arguments:
- grid_values: bfloat16 [1024, 64, 5376], P('wa', 'vert'), may hold values from -6 to 6
- row_length: int32 [1024], P('wa'), may hold values from 20 to 5136, as said below
- pair_order: int32 [640], replicated, may hold values from 0 to 639, each once
- legendre: bfloat16 [640, 512, 1281], P(('wa', 'vert')), may hold values from -0.25 to 0.25
Outputs:
- spectral: float32 [640, 2, 64, 1281], P(('wa', 'vert'))
Inputs may be any that keep to these rules, and one draw needn't show every extreme that they name: `row_length`: row r and row 512 + r have the same length; the first 512 lengths are 20 + 4 j for distinct j, strictly increasing, and the last of them is 5136. `pair_order`: every pair stands in exactly one slot.
All inputs are finite; a program needn't handle non-finite values.
Results may differ from a plain program's by a relative error of at most 0.0048.
Values may be sent and summed in bfloat16 or wider, within the bound.
A program may use at most 128 MiB of HBM per device.

v0:
```python
import math

import jax
import jax.numpy as jnp
from jax import lax
from jax.sharding import PartitionSpec as P

TRUNC = 1279
SUB = 256
LPAD = 5376


def for_sending(value):

    def short(part):
        return part.astype(jnp.bfloat16) if part.dtype == jnp.float32 else part

    return jax.tree.map(short, value)


def partner_2(value, axis, distance):
    return lax.ppermute(value, axis, [(i, i ^ 1 << distance) for i in range(lax.axis_size(axis))])


def row_tables(length):
    wave_ids = jnp.arange(TRUNC + 1, dtype=jnp.int32)
    points = jnp.arange(SUB, dtype=jnp.int32)
    blocks = jnp.arange(LPAD // SUB, dtype=jnp.int32)
    length_float = length.astype(jnp.float32)
    step_angle = 2.0 * math.pi / length_float
    inner_angle = (points[:, None] * wave_ids[None, :] % length).astype(jnp.float32) * step_angle
    inner_table = jnp.concatenate([jnp.cos(inner_angle), -jnp.sin(inner_angle)], axis=1).astype(
        jnp.bfloat16
    )
    outer_angle = (blocks[:, None] * (SUB * wave_ids)[None, :] % length).astype(
        jnp.float32
    ) * step_angle
    keep_scale = (wave_ids <= (length - 1) // 2).astype(jnp.float32) / jnp.sqrt(length_float)
    return (inner_table, jnp.cos(outer_angle), -jnp.sin(outer_angle), keep_scale)


def masked_row(grid_row, length):
    valid = jnp.arange(LPAD, dtype=jnp.int32) < length
    return jnp.where(valid[None, :], grid_row, jnp.zeros_like(grid_row))


def padded_row(row_item):
    grid_row, length = row_item
    inner_table, twist_cos, twist_sin, keep_scale = row_tables(length)
    field_count = grid_row.shape[0]
    block_total = LPAD // SUB
    wave_total = TRUNC + 1
    masked = masked_row(grid_row, length)
    partial_value = jnp.dot(
        masked.reshape(field_count * block_total, SUB),
        inner_table,
        preferred_element_type=jnp.float32,
    )
    partial_value = partial_value.reshape(field_count, block_total, 2 * wave_total)
    cos_part = partial_value[:, :, :wave_total]
    sin_part = partial_value[:, :, wave_total:]
    real_part = jnp.sum(cos_part * twist_cos - sin_part * twist_sin, axis=1) * keep_scale
    imag_part = jnp.sum(cos_part * twist_sin + sin_part * twist_cos, axis=1) * keep_scale
    return jnp.stack([real_part, imag_part], axis=1).astype(jnp.bfloat16)


def legendre_apply(sym_part, anti_part, leg_table, local_pairs, perm):
    half_wa, first_dim, second_dim, field_dev, _unused, col_total = sym_part.shape
    slot_count = leg_table.shape[0]
    lat_pairs = leg_table.shape[1]
    col_count = leg_table.shape[2]
    field_count = first_dim * second_dim * field_dev // (lat_pairs // half_wa)
    sym_seven = sym_part.reshape(half_wa, first_dim, second_dim, field_dev, 2, slot_count, 2)
    anti_seven = anti_part.reshape(half_wa, first_dim, second_dim, field_dev, 2, slot_count, 2)
    stacked = jnp.stack([sym_seven, anti_seven], axis=0)
    operand = jnp.transpose(stacked, perm).reshape(slot_count, lat_pairs, 8 * field_count)
    product = lax.dot_general(
        leg_table, operand, (((1,), (1,)), ((0,), (0,))), preferred_element_type=jnp.float32
    )
    product = product.reshape(slot_count, col_count, 4, 2, field_count)
    column = jnp.arange(col_count, dtype=jnp.int32)
    first_count = TRUNC + 1 - local_pairs
    in_first = column[None, :] < first_count[:, None]
    degree = jnp.where(in_first, column[None, :], column[None, :] - first_count[:, None])
    group_idx = jnp.where(in_first, 0, 2) + degree % 2
    pick_mask = (group_idx[:, :, None] == jnp.arange(4, dtype=jnp.int32)[None, None, :]).astype(
        jnp.float32
    )
    chosen = jnp.sum(product * pick_mask[:, :, :, None, None], axis=2)
    return jnp.transpose(chosen, (0, 2, 3, 1))


def body(grid_values, row_length, pair_order, legendre):
    fourier = lax.map(padded_row, (grid_values, row_length), batch_size=2)
    col_ids = jnp.stack([pair_order, TRUNC - pair_order], axis=1).reshape(-1)
    ordered = jnp.take(fourier, col_ids, axis=3)
    wa_count = lax.axis_size("wa")
    vert_count = lax.axis_size("vert")
    half_wa = wa_count // 2
    north_side = lax.axis_index("wa") < half_wa
    partner = partner_2(for_sending(ordered), "wa", wa_count.bit_length() - 2).astype(ordered.dtype)
    own_wide = ordered.astype(jnp.float32)
    other_wide = partner.astype(jnp.float32)
    outgoing = jnp.where(north_side, own_wide + other_wide, other_wide - own_wide).astype(
        jnp.bfloat16
    )
    row_count = outgoing.shape[0]
    field_dev = outgoing.shape[1]
    joined = lax.all_to_all(outgoing, ("wa", "vert"), split_axis=3, concat_axis=0, tiled=True)
    slot_cols = joined.shape[3]
    split_at = half_wa * vert_count * row_count
    north_rows = joined[:split_at].reshape(half_wa, vert_count, row_count, field_dev, 2, slot_cols)
    south_rows = joined[split_at:].reshape(half_wa, vert_count, row_count, field_dev, 2, slot_cols)
    perm = (6, 1, 3, 7, 0, 5, 2, 4)
    slot_count = legendre.shape[0]
    owner_idx = lax.axis_index("wa") * vert_count + lax.axis_index("vert")
    local_pairs = lax.dynamic_slice_in_dim(pair_order, owner_idx * slot_count, slot_count)
    return legendre_apply(north_rows, south_rows, legendre, local_pairs, perm)


def solution(mesh):
    placed = (P("wa", "vert", None), P("wa"), P(), P(("wa", "vert"), None, None))
    return jax.shard_map(
        body,
        mesh=mesh,
        in_specs=placed,
        out_specs=P(("wa", "vert"), None, None, None),
        check_vma=False,
    )
```

profile of v0, /device:TPU:1, one launch (start us, length us, event | category | flops | bytes accessed | tf_op | source)
XLA Modules:
  0.0 1465.4 jit_solution(11926932633173966053)
XLA Ops:
  2.8 1137.8 %while.13 = (s32[]{:T(128)}, bf16[16,2,16,2,1280]{4,2,3,1,0:T(8,128)(2,1)}, s32[16,2]{1,0:T(8,128)S(1)}, bf16[16,2,16,5376]{3,2,1,0:T(8,128)(2,1)}, s32[]{:T(128)}) while((s32[]{:T(128)}, bf16[16,2,16,2,1280]{4,2,3,1,0:T(8,128)(2,1)}, s32[16,2]{1,0:T(8,128)S(1)}, bf16[16,2,16,5376]{3,2,1,0:T(8,128)(2,1)}, s32[]{:T(128)}) %tuple.51), condition=%wide.region_3.4_spmd, body=%wide.region_0.3_spmd.sunk | while | flops 902040128 | bytes 40400584 | solution.py:94
  3.0 34.5 %fusion.46 = (bf16[2,256,1280]{2,1,0:T(8,128)(2,1)S(1)}, bf16[2,256,1280]{2,1,0:T(8,128)(2,1)S(1)}) fusion(f32[2]{0:T(128)S(1)} %get-tuple-element.136, s32[2]{0:T(128)S(1)} %compare_select_fusion.7, s32[256,1280]{1,0:T(8,128)S(1)} %iota_multiply_fusion.6, pred[2]{0:T(512)(128)(4,1)S(1)} %broadcast_compare_fusion.2), kind=kLoop, calls=%fused_computation.11.clone.1 | loop fusion | flops 7864320 | bytes 3932178 | tf_op jit(solution)/shard_map/convert.4
  43.4 11.1 copy.50
  54.6 11.6 fusion.48
  74.0 34.5 %fusion.46 = (bf16[2,256,1280]{2,1,0:T(8,128)(2,1)S(1)}, bf16[2,256,1280]{2,1,0:T(8,128)(2,1)S(1)}) fusion(f32[2]{0:T(128)S(1)} %get-tuple-element.136, s32[2]{0:T(128)S(1)} %compare_select_fusion.7, s32[256,1280]{1,0:T(8,128)S(1)} %iota_multiply_fusion.6, pred[2]{0:T(512)(128)(4,1)S(1)} %broadcast_compare_fusion.2), kind=kLoop, calls=%fused_computation.11.clone.1 | loop fusion | flops 7864320 | bytes 3932178 | tf_op jit(solution)/shard_map/convert.4
  114.5 11.1 copy.50
  125.7 11.6 fusion.48
  145.1 34.5 %fusion.46 = (bf16[2,256,1280]{2,1,0:T(8,128)(2,1)S(1)}, bf16[2,256,1280]{2,1,0:T(8,128)(2,1)S(1)}) fusion(f32[2]{0:T(128)S(1)} %get-tuple-element.136, s32[2]{0:T(128)S(1)} %compare_select_fusion.7, s32[256,1280]{1,0:T(8,128)S(1)} %iota_multiply_fusion.6, pred[2]{0:T(512)(128)(4,1)S(1)} %broadcast_compare_fusion.2), kind=kLoop, calls=%fused_computation.11.clone.1 | loop fusion | flops 7864320 | bytes 3932178 | tf_op jit(solution)/shard_map/convert.4
  185.6 11.1 copy.50
  196.7 11.6 fusion.48
  216.2 34.5 %fusion.46 = (bf16[2,256,1280]{2,1,0:T(8,128)(2,1)S(1)}, bf16[2,256,1280]{2,1,0:T(8,128)(2,1)S(1)}) fusion(f32[2]{0:T(128)S(1)} %get-tuple-element.136, s32[2]{0:T(128)S(1)} %compare_select_fusion.7, s32[256,1280]{1,0:T(8,128)S(1)} %iota_multiply_fusion.6, pred[2]{0:T(512)(128)(4,1)S(1)} %broadcast_compare_fusion.2), kind=kLoop, calls=%fused_computation.11.clone.1 | loop fusion | flops 7864320 | bytes 3932178 | tf_op jit(solution)/shard_map/convert.4
  267.8 11.6 fusion.48
  287.3 34.5 %fusion.46 = (bf16[2,256,1280]{2,1,0:T(8,128)(2,1)S(1)}, bf16[2,256,1280]{2,1,0:T(8,128)(2,1)S(1)}) fusion(f32[2]{0:T(128)S(1)} %get-tuple-element.136, s32[2]{0:T(128)S(1)} %compare_select_fusion.7, s32[256,1280]{1,0:T(8,128)S(1)} %iota_multiply_fusion.6, pred[2]{0:T(512)(128)(4,1)S(1)} %broadcast_compare_fusion.2), kind=kLoop, calls=%fused_computation.11.clone.1 | loop fusion | flops 7864320 | bytes 3932178 | tf_op jit(solution)/shard_map/convert.4
  338.9 11.6 fusion.48
  358.4 34.5 %fusion.46 = (bf16[2,256,1280]{2,1,0:T(8,128)(2,1)S(1)}, bf16[2,256,1280]{2,1,0:T(8,128)(2,1)S(1)}) fusion(f32[2]{0:T(128)S(1)} %get-tuple-element.136, s32[2]{0:T(128)S(1)} %compare_select_fusion.7, s32[256,1280]{1,0:T(8,128)S(1)} %iota_multiply_fusion.6, pred[2]{0:T(512)(128)(4,1)S(1)} %broadcast_compare_fusion.2), kind=kLoop, calls=%fused_computation.11.clone.1 | loop fusion | flops 7864320 | bytes 3932178 | tf_op jit(solution)/shard_map/convert.4
  410.0 11.6 fusion.48
  429.5 34.5 %fusion.46 = (bf16[2,256,1280]{2,1,0:T(8,128)(2,1)S(1)}, bf16[2,256,1280]{2,1,0:T(8,128)(2,1)S(1)}) fusion(f32[2]{0:T(128)S(1)} %get-tuple-element.136, s32[2]{0:T(128)S(1)} %compare_select_fusion.7, s32[256,1280]{1,0:T(8,128)S(1)} %iota_multiply_fusion.6, pred[2]{0:T(512)(128)(4,1)S(1)} %broadcast_compare_fusion.2), kind=kLoop, calls=%fused_computation.11.clone.1 | loop fusion | flops 7864320 | bytes 3932178 | tf_op jit(solution)/shard_map/convert.4
  481.1 11.6 fusion.48
  500.6 34.5 %fusion.46 = (bf16[2,256,1280]{2,1,0:T(8,128)(2,1)S(1)}, bf16[2,256,1280]{2,1,0:T(8,128)(2,1)S(1)}) fusion(f32[2]{0:T(128)S(1)} %get-tuple-element.136, s32[2]{0:T(128)S(1)} %compare_select_fusion.7, s32[256,1280]{1,0:T(8,128)S(1)} %iota_multiply_fusion.6, pred[2]{0:T(512)(128)(4,1)S(1)} %broadcast_compare_fusion.2), kind=kLoop, calls=%fused_computation.11.clone.1 | loop fusion | flops 7864320 | bytes 3932178 | tf_op jit(solution)/shard_map/convert.4
  552.2 11.6 fusion.48
  571.7 34.5 %fusion.46 = (bf16[2,256,1280]{2,1,0:T(8,128)(2,1)S(1)}, bf16[2,256,1280]{2,1,0:T(8,128)(2,1)S(1)}) fusion(f32[2]{0:T(128)S(1)} %get-tuple-element.136, s32[2]{0:T(128)S(1)} %compare_select_fusion.7, s32[256,1280]{1,0:T(8,128)S(1)} %iota_multiply_fusion.6, pred[2]{0:T(512)(128)(4,1)S(1)} %broadcast_compare_fusion.2), kind=kLoop, calls=%fused_computation.11.clone.1 | loop fusion | flops 7864320 | bytes 3932178 | tf_op jit(solution)/shard_map/convert.4
  623.3 11.6 fusion.48
  642.8 34.5 %fusion.46 = (bf16[2,256,1280]{2,1,0:T(8,128)(2,1)S(1)}, bf16[2,256,1280]{2,1,0:T(8,128)(2,1)S(1)}) fusion(f32[2]{0:T(128)S(1)} %get-tuple-element.136, s32[2]{0:T(128)S(1)} %compare_select_fusion.7, s32[256,1280]{1,0:T(8,128)S(1)} %iota_multiply_fusion.6, pred[2]{0:T(512)(128)(4,1)S(1)} %broadcast_compare_fusion.2), kind=kLoop, calls=%fused_computation.11.clone.1 | loop fusion | flops 7864320 | bytes 3932178 | tf_op jit(solution)/shard_map/convert.4
  694.4 11.6 fusion.48
  713.9 34.5 %fusion.46 = (bf16[2,256,1280]{2,1,0:T(8,128)(2,1)S(1)}, bf16[2,256,1280]{2,1,0:T(8,128)(2,1)S(1)}) fusion(f32[2]{0:T(128)S(1)} %get-tuple-element.136, s32[2]{0:T(128)S(1)} %compare_select_fusion.7, s32[256,1280]{1,0:T(8,128)S(1)} %iota_multiply_fusion.6, pred[2]{0:T(512)(128)(4,1)S(1)} %broadcast_compare_fusion.2), kind=kLoop, calls=%fused_computation.11.clone.1 | loop fusion | flops 7864320 | bytes 3932178 | tf_op jit(solution)/shard_map/convert.4
  765.5 11.6 fusion.48
  784.9 34.5 %fusion.46 = (bf16[2,256,1280]{2,1,0:T(8,128)(2,1)S(1)}, bf16[2,256,1280]{2,1,0:T(8,128)(2,1)S(1)}) fusion(f32[2]{0:T(128)S(1)} %get-tuple-element.136, s32[2]{0:T(128)S(1)} %compare_select_fusion.7, s32[256,1280]{1,0:T(8,128)S(1)} %iota_multiply_fusion.6, pred[2]{0:T(512)(128)(4,1)S(1)} %broadcast_compare_fusion.2), kind=kLoop, calls=%fused_computation.11.clone.1 | loop fusion | flops 7864320 | bytes 3932178 | tf_op jit(solution)/shard_map/convert.4
  836.6 11.6 fusion.48
  856.0 34.5 %fusion.46 = (bf16[2,256,1280]{2,1,0:T(8,128)(2,1)S(1)}, bf16[2,256,1280]{2,1,0:T(8,128)(2,1)S(1)}) fusion(f32[2]{0:T(128)S(1)} %get-tuple-element.136, s32[2]{0:T(128)S(1)} %compare_select_fusion.7, s32[256,1280]{1,0:T(8,128)S(1)} %iota_multiply_fusion.6, pred[2]{0:T(512)(128)(4,1)S(1)} %broadcast_compare_fusion.2), kind=kLoop, calls=%fused_computation.11.clone.1 | loop fusion | flops 7864320 | bytes 3932178 | tf_op jit(solution)/shard_map/convert.4
  907.6 11.6 fusion.48
  927.1 34.5 %fusion.46 = (bf16[2,256,1280]{2,1,0:T(8,128)(2,1)S(1)}, bf16[2,256,1280]{2,1,0:T(8,128)(2,1)S(1)}) fusion(f32[2]{0:T(128)S(1)} %get-tuple-element.136, s32[2]{0:T(128)S(1)} %compare_select_fusion.7, s32[256,1280]{1,0:T(8,128)S(1)} %iota_multiply_fusion.6, pred[2]{0:T(512)(128)(4,1)S(1)} %broadcast_compare_fusion.2), kind=kLoop, calls=%fused_computation.11.clone.1 | loop fusion | flops 7864320 | bytes 3932178 | tf_op jit(solution)/shard_map/convert.4
  978.7 11.6 fusion.48
  998.2 34.5 %fusion.46 = (bf16[2,256,1280]{2,1,0:T(8,128)(2,1)S(1)}, bf16[2,256,1280]{2,1,0:T(8,128)(2,1)S(1)}) fusion(f32[2]{0:T(128)S(1)} %get-tuple-element.136, s32[2]{0:T(128)S(1)} %compare_select_fusion.7, s32[256,1280]{1,0:T(8,128)S(1)} %iota_multiply_fusion.6, pred[2]{0:T(512)(128)(4,1)S(1)} %broadcast_compare_fusion.2), kind=kLoop, calls=%fused_computation.11.clone.1 | loop fusion | flops 7864320 | bytes 3932178 | tf_op jit(solution)/shard_map/convert.4
  1049.8 11.6 fusion.48
  1069.3 34.5 %fusion.46 = (bf16[2,256,1280]{2,1,0:T(8,128)(2,1)S(1)}, bf16[2,256,1280]{2,1,0:T(8,128)(2,1)S(1)}) fusion(f32[2]{0:T(128)S(1)} %get-tuple-element.136, s32[2]{0:T(128)S(1)} %compare_select_fusion.7, s32[256,1280]{1,0:T(8,128)S(1)} %iota_multiply_fusion.6, pred[2]{0:T(512)(128)(4,1)S(1)} %broadcast_compare_fusion.2), kind=kLoop, calls=%fused_computation.11.clone.1 | loop fusion | flops 7864320 | bytes 3932178 | tf_op jit(solution)/shard_map/convert.4
  1120.9 11.6 fusion.48
  1140.6 15.6 %copy.33 = bf16[32,16,2,1280]{0,1,3,2:T(8,128)(2,1)} copy(bf16[32,16,2,1280]{3,1,2,0:T(8,128)(2,1)} %bitcast.60) | data formatting | bytes 5242880 | tf_op jit(solution)/shard_map/reshape | solution.py:94
  1166.6 11.7 select_bitcast_fusion
  1178.3 13.4 copy.34
  1195.4 56.2 %collective-permute-done = bf16[32,16,2,1280]{3,1,2,0:T(8,128)(2,1)} collective-permute-done((bf16[32,16,2,1280]{3,1,2,0:T(8,128)(2,1)S(1)}, bf16[32,16,2,1280]{3,1,2,0:T(8,128)(2,1)}, u32[]{:S(2)}, u32[]{:S(2)}) %collective-permute-start) | collective-permute-done | bytes 2621472 | tf_op jit(solution)/shard_map/ppermute | solution.py:22
  1251.6 18.5 %copy.35 = bf16[32,16,2,1280]{0,1,2,3:T(8,128)(2,1)} copy(bf16[32,16,2,1280]{3,1,2,0:T(8,128)(2,1)} %collective-permute-done) | data formatting | bytes 5242880 | tf_op jit(solution)/shard_map/ppermute | solution.py:22
  1270.0 14.7 %fusion.34 = bf16[1280,2,16,32]{3,2,1,0:T(8,128)(2,1)} fusion(bf16[32,16,2,1280]{0,1,2,3:T(8,128)(2,1)} %copy.35, pred[]{:T(512)S(6)} %lt.123, bf16[1280,32,16,2]{1,2,3,0:T(8,128)(2,1)} %gather_fusion, pred[1280]{0:T(1024)(128)(4,1)S(1)} %compare_and_fusion), kind=kLoop, calls=%fused_computation.79 | loop fusion | flops 9175040 | bytes 7865601
  1284.7 15.9 %reshape.388 = bf16[128,2,5120]{2,1,0:T(2,128)(2,1)} reshape(bf16[1280,2,16,32]{3,2,1,0:T(8,128)(2,1)} %fusion.34) | data formatting | bytes 5242880
  1300.6 11.9 all-to-all-start
  1313.5 35.5 %all-to-all-done = bf16[128,2,5120]{2,1,0:T(2,128)(2,1)S(1)} async-done(((bf16[128,2,5120]{2,1,0:T(2,128)(2,1)}), bf16[128,2,5120]{2,1,0:T(2,128)(2,1)S(1)}, u32[]{:S(2)}, u32[]{:S(2)}) %all-to-all-start) | async-done | bytes 2621472 | tf_op jit(solution)/shard_map/all_to_all | solution.py:109
  1398.3 20.2 %copy.39 = bf16[5,16,32,2,2,2,4,16]{2,1,7,6,5,4,3,0:T(8,128)(2,1)} copy(bf16[5,16,32,2,2,2,4,16]{2,7,3,0,5,6,1,4:T(8,128)(2,1)} %maximum_bitcast_fusion) | data formatting | bytes 5242880 | tf_op jit(solution)/shard_map/transpose | solution.py:76
  1418.5 13.4 reshape.377
  1441.6 14.4 copy.41
  (328 shorter events, 450.2 us)
Async XLA Ops:
  1191.7 59.9 %collective-permute-start = (bf16[32,16,2,1280]{3,1,2,0:T(8,128)(2,1)S(1)}, bf16[32,16,2,1280]{3,1,2,0:T(8,128)(2,1)}, u32[]{:S(2)}, u32[]{:S(2)}) collective-permute-start(bf16[32,16,2,1280]{3,1,2,0:T(8,128)(2,1)S(1)} %copy.34), channel_id=1, source_target_pairs={{0,64},{4,68},{8,72},{12,76},{16,80},{20,84},{24,88},{28,92},{32,9... | collective-permute-start | bytes 7864328 | tf_op jit(solution)/shard_map/ppermute | solution.py:22
  1300.6 48.4 %all-to-all-start = ((bf16[128,2,5120]{2,1,0:T(2,128)(2,1)}), bf16[128,2,5120]{2,1,0:T(2,128)(2,1)S(1)}, u32[]{:S(2)}, u32[]{:S(2)}) async-start(bf16[128,2,5120]{2,1,0:T(2,128)(2,1)} %reshape.388), calls=%async_computation | async-start | bytes 5242880 | tf_op jit(solution)/shard_map/all_to_all | solution.py:109
  1377.1 6.8 copy-start
where the time goes:
time: 1480 us; the launch traced here: 1470 us
  other arithmetic  901 us (61%)
  local copies, waits for them, and re-layouts  383 us (26%)
  waiting for transfers between devices  91.8 us (6%)
  matrix products  71.7 us (5%)
  starting transfers between devices  15.6 us (1%)
    another operation x16, other arithmetic  552 us
    cos x16, other arithmetic, row_tables(): jnp.cos(outer_angle)  186 us
    dot_general x16, local copies, waits for them, and re-layouts, padded_row(): jnp.dot(masked.reshape(field_count * block_total, SUB), inner_table, pref...  178 us
    reduce_sum x16, other arithmetic, padded_row(): jnp.sum(cos_part * twist_cos - sin_part * twist_sin, axis=1) * keep_scale  105 us
    dot_general x16, matrix products, padded_row(): jnp.dot(masked.reshape(field_count * block_total, SUB), inner_table, pref...  62 us
    ppermute x1, waiting for transfers between devices, partner_2(): lax.ppermute(value, axis, [(i, i ^ 1 << distance) for i in range(lax.axis...  56.2 us
    all_to_all x1, waiting for transfers between devices, body(): lax.all_to_all(outgoing, ('wa', 'vert'), split_axis=3, concat_axis=0, til...  35.5 us
  transfers between devices with their start and end apart: 2, of which 2 were waited for; matrix products, arithmetic and copies ran while one was open for 0% of the time, Pallas kernels for 0%

commit v1 on v0

v1 whole, which is shorter than its diff:
```python
import functools
import math

import jax
import jax.numpy as jnp
from jax import lax
from jax.experimental import pallas as pl
from jax.experimental.pallas import tpu as pltpu
from jax.sharding import PartitionSpec as P

TRUNC = 1279
SUB = 256
LPAD = 5376
WAVES = TRUNC + 1
CLASS = WAVES // 4
CPAD = 384
LANE = 128
CHUNKS = 11
BLOCKS = 6
GROUPS = 8
SPAN = 4


def sincos(turns):
    quarter = turns * 4.0
    near = jnp.floor(quarter + 0.5)
    f = quarter - near
    f2 = f * f
    h = math.pi / 2
    s = f * (h + f2 * (-(h**3) / 6 + f2 * (h**5 / 120 + f2 * (-(h**7) / 5040 + f2 * (h**9 / 362880)))))
    c = 1.0 + f2 * (
        -(h**2) / 2 + f2 * (h**4 / 24 + f2 * (-(h**6) / 720 + f2 * (h**8 / 40320 - f2 * (h**10 / 3628800))))
    )
    which = near - 4.0 * jnp.floor(near * 0.25)
    odd = (which == 1.0) | (which == 3.0)
    cos_out = jnp.where(odd, s, c)
    sin_out = jnp.where(odd, c, s)
    cos_out = jnp.where((which == 1.0) | (which == 2.0), -cos_out, cos_out)
    sin_out = jnp.where(which >= 2.0, -sin_out, sin_out)
    return cos_out, sin_out


def turns_of(product, n_float, inv_n):
    return (product - jnp.floor(product * inv_n) * n_float) * inv_n


def iota_f(shape, dim):
    return lax.broadcasted_iota(jnp.int32, shape, dim).astype(jnp.float32)


def fourier_kernel(quarter_ref, inv_ref, scale_ref, grid_ref, order_ref, out_ref, lhs, rhs, tens, onehot, rows, spread):
    g = pl.program_id(0)

    @pl.when(g == 0)
    def _():
        lhs[...] = jnp.zeros_like(lhs)
        for r in range(4):
            wave = lax.broadcasted_iota(jnp.int32, (WAVES, CPAD), 1) * 4 + r
            wave = jnp.where(wave < WAVES, wave, -1)
            onehot[:, r * CPAD : (r + 1) * CPAD] = (wave == order_ref[...]).astype(jnp.float32).astype(jnp.bfloat16)

    def one_row(t, carry):
        row = t * GROUPS + g
        n = quarter_ref[row]
        inv_n = inv_ref[row]
        scale = scale_ref[row]
        n_float = n.astype(jnp.float32)

        u = iota_f((8, CPAD), 1)
        low = iota_f((8, CPAD), 0)
        base = []
        for half in range(2):
            c, s = sincos(turns_of((low + 8.0 * half) * u, n_float, inv_n))
            base.append((c, s))
            c, s = sincos(turns_of((low + 8.0 * half) * 16.0 * u, n_float, inv_n))
            tens[0, half * 8 : half * 8 + 8] = c
            tens[1, half * 8 : half * 8 + 8] = s
        for a in range(16):
            ca = tens[0, a : a + 1, :]
            sa = tens[1, a : a + 1, :]
            c = jnp.concatenate([cb * ca - sb * sa for cb, sb in base], axis=0)
            s = jnp.concatenate([sb * ca + cb * sa for cb, sb in base], axis=0)
            c16 = c.astype(jnp.bfloat16)
            s16 = s.astype(jnp.bfloat16)
            rhs[a * 16 : a * 16 + 16, :CPAD] = c16
            rhs[a * 16 : a * 16 + 16, CPAD:] = (-s).astype(jnp.bfloat16)
            rhs[SUB + a * 16 : SUB + a * 16 + 16, :CPAD] = s16
            rhs[SUB + a * 16 : SUB + a * 16 + 16, CPAD:] = c16

        lane = lax.broadcasted_iota(jnp.int32, (16, LANE), 1)
        quarters = []
        for part in range(4):
            start = n * part
            whole = start // LANE
            shift = start - whole * LANE
            count = CHUNKS + (1 if part else 0)
            pieces = [
                grid_ref[t, 0, :, pl.ds(pl.multiple_of((whole + j) * LANE, LANE), LANE)].astype(jnp.float32)
                for j in range(count)
            ]
            if part:
                back = lax.rem(LANE - shift, LANE)
                turned = [pltpu.roll(piece, back, 1) for piece in pieces]
                keep = lane < LANE - shift
                pieces = [jnp.where(keep, turned[j], turned[j + 1]) for j in range(CHUNKS)]
            quarters.append(pieces)

        lane8 = lax.broadcasted_iota(jnp.int32, (8, LANE), 1)
        for j in range(CHUNKS):
            k = lane8 + j * LANE
            inside = k < n
            c1, s1 = sincos(k.astype(jnp.float32) * (inv_n * 0.25))
            c2 = c1 * c1 - s1 * s1
            s2 = 2.0 * c1 * s1
            c3 = c2 * c1 - s2 * s1
            s3 = s2 * c1 + c2 * s1

            def both(v):
                v = jnp.where(inside, v, 0.0)
                return jnp.concatenate([v, v], axis=0)

            c1, s1, c2, s2, c3, s3 = (both(v) for v in (c1, s1, c2, s2, c3, s3))
            qa, qb, qc, qd = (quarters[part][j] for part in range(4))
            even = qa + qc
            even_other = qb + qd
            re = qa - qc
            im = qd - qb
            h0 = jnp.where(lane + j * LANE < n, even + even_other, 0.0)
            h2 = even - even_other
            values = (
                (h0, None),
                (re * c1 + im * s1, im * c1 - re * s1),
                (h2 * c2, -(h2 * s2)),
                (re * c3 - im * s3, -(im * c3 + re * s3)),
            )
            q = j // 2
            at = (j % 2) * LANE
            for r, (zr, zi) in enumerate(values):
                top = (r * BLOCKS + q) * 16
                lhs[top : top + 16, at : at + LANE] = zr.astype(jnp.bfloat16)
                if zi is not None:
                    lhs[top : top + 16, SUB + at : SUB + at + LANE] = zi.astype(jnp.bfloat16)

        part_sum = jnp.dot(lhs[...], rhs[...], preferred_element_type=jnp.float32)

        tc, ts = sincos(turns_of(low * 256.0 * u, n_float, inv_n))
        column = lax.broadcasted_iota(jnp.int32, (1, CPAD), 1)
        lane_top = pl.multiple_of((g % 2) * LANE + t * 32, 32)
        for r in range(4):
            real = part_sum[r * 96 : r * 96 + 16, :CPAD]
            imag = part_sum[r * 96 : r * 96 + 16, CPAD:]
            for q in range(1, BLOCKS):
                top = r * 96 + q * 16
                pr = part_sum[top : top + 16, :CPAD]
                pi = part_sum[top : top + 16, CPAD:]
                c = tc[q : q + 1, :]
                s = ts[q : q + 1, :]
                real = real + (pr * c + pi * s)
                imag = imag + (pi * c - pr * s)
            wave = column * 4 + r
            keep = jnp.where((wave <= 2 * n - 1) & (column < CLASS), scale, 0.0)
            rows[pl.ds(lane_top, 16), r * CPAD : (r + 1) * CPAD] = (real * keep).astype(jnp.bfloat16)
            rows[pl.ds(lane_top + 16, 16), r * CPAD : (r + 1) * CPAD] = (imag * keep).astype(jnp.bfloat16)
        return carry

    lax.fori_loop(0, SPAN, one_row, 0)

    @pl.when(g % 2 == 1)
    def _():
        step = 256

        def order(i, carry):
            top = pl.multiple_of(i * step, step)
            picked = lax.dot_general(
                onehot[pl.ds(top, step), :],
                rows[...],
                (((1,), (1,)), ((), ())),
                preferred_element_type=jnp.float32,
            )
            spread[pl.ds(top * GROUPS + g - 1, step, stride=GROUPS), :] = picked[:, :LANE]
            spread[pl.ds(top * GROUPS + g, step, stride=GROUPS), :] = picked[:, LANE:]
            return carry

        lax.fori_loop(0, WAVES // step, order, 0)

    @pl.when(g == GROUPS - 1)
    def _():
        dest_rows = out_ref.shape[1]

        def finish(d, carry):
            out_ref[d] = spread[pl.ds(pl.multiple_of(d * dest_rows, dest_rows), dest_rows), :].astype(jnp.bfloat16)
            return carry

        lax.fori_loop(0, out_ref.shape[0], finish, 0)


def fourier_all(grid_values, row_length, order, device_total):
    row_total, field_count, points = grid_values.shape
    quarter = row_length // 4
    length_float = row_length.astype(jnp.float32)
    inv_n = 1.0 / quarter.astype(jnp.float32)
    scale = 1.0 / jnp.sqrt(length_float)
    smem = pl.BlockSpec(memory_space=pltpu.SMEM)
    dest_rows = WAVES * GROUPS // device_total
    return pl.pallas_call(
        fourier_kernel,
        grid=(GROUPS,),
        in_specs=[
            smem,
            smem,
            smem,
            pl.BlockSpec((SPAN, 1, field_count, points), lambda g: (0, g, 0, 0)),
            pl.BlockSpec((WAVES, 1), lambda g: (0, 0)),
        ],
        out_specs=pl.BlockSpec((device_total, dest_rows, LANE), lambda g: (0, 0, 0)),
        out_shape=jax.ShapeDtypeStruct((device_total, dest_rows, LANE), jnp.bfloat16),
        scratch_shapes=[
            pltpu.VMEM((4 * BLOCKS * 16, 2 * SUB), jnp.bfloat16),
            pltpu.VMEM((2 * SUB, 2 * CPAD), jnp.bfloat16),
            pltpu.VMEM((2, 16, CPAD), jnp.float32),
            pltpu.VMEM((WAVES, 4 * CPAD), jnp.bfloat16),
            pltpu.VMEM((2 * LANE, 4 * CPAD), jnp.bfloat16),
            pltpu.VMEM((WAVES * GROUPS, LANE), jnp.float32),
        ],
        compiler_params=pltpu.CompilerParams(vmem_limit_bytes=48 * 2**20),
        name="fourier",
    )(quarter, inv_n, scale, grid_values.reshape(SPAN, GROUPS, field_count, points), order.reshape(WAVES, 1))


def legendre_kernel(first_ref, recv_ref, leg_ref, out_ref, operand):
    slot = pl.program_id(0)
    lane = lax.broadcasted_iota(jnp.int32, (16, LANE), 1)
    odd32 = (lane // 32) % 2 == 1
    high64 = lane >= 64

    def regroup(tiles):
        a, b, c, d = tiles
        ab0 = jnp.where(odd32, pltpu.roll(b, 32, 1), a)
        ab1 = jnp.where(odd32, b, pltpu.roll(a, 96, 1))
        cd0 = jnp.where(odd32, pltpu.roll(d, 32, 1), c)
        cd1 = jnp.where(odd32, d, pltpu.roll(c, 96, 1))
        return (
            jnp.where(high64, pltpu.roll(cd0, 64, 1), ab0),
            jnp.where(high64, pltpu.roll(cd1, 64, 1), ab1),
            jnp.where(high64, cd0, pltpu.roll(ab0, 64, 1)),
            jnp.where(high64, cd1, pltpu.roll(ab1, 64, 1)),
        )

    half = recv_ref.shape[0] // 2

    def pair(w, carry):
        north = regroup([recv_ref[w, v, 0].astype(jnp.float32) for v in range(4)])
        south = regroup([recv_ref[half + w, v, 0].astype(jnp.float32) for v in range(4)])
        for t in range(0, 4, 2):
            top = pl.multiple_of(w * 32 + t * 8, 16)
            sums = [north[t + e] + south[t + e] for e in range(2)]
            differences = [north[t + e] - south[t + e] for e in range(2)]
            for side in range(2):
                rows = slice(side * 8, side * 8 + 8)
                for kind, both in enumerate((sums, differences)):
                    at = (side * 2 + kind) * LANE
                    operand[pl.ds(top, 16), at : at + LANE] = jnp.concatenate(
                        [both[0][rows], both[1][rows]], axis=0
                    ).astype(jnp.bfloat16)
        return carry

    lax.fori_loop(0, half, pair, 0)
    first_count = first_ref[slot]
    columns = leg_ref.shape[2]
    product = lax.dot_general(
        operand[...], leg_ref[0], (((0,), (0,)), ((), ())), preferred_element_type=jnp.float32
    )
    column = lax.broadcasted_iota(jnp.int32, (1, columns), 1)
    in_first = column < first_count
    degree = jnp.where(in_first, column, column - first_count)
    even = degree % 2 == 0
    for v in range(4):
        for i in range(2):
            top = v * 32 + i * 16
            s0, a0, s1, a1 = (product[k * LANE + top : k * LANE + top + 16] for k in range(4))
            chosen = jnp.where(in_first, jnp.where(even, s0, a0), jnp.where(even, s1, a1))
            out_ref[0, i, v * 16 : v * 16 + 16, :] = chosen


def legendre_all(received, legendre, local_pairs, wa_count, vert_count):
    slot_count, lat_pairs, columns = legendre.shape
    field_count = 16 * vert_count
    first_count = (WAVES - local_pairs).astype(jnp.int32)
    shaped = received.reshape(wa_count, vert_count, slot_count, 16, LANE)
    return pl.pallas_call(
        legendre_kernel,
        grid=(slot_count,),
        in_specs=[
            pl.BlockSpec(memory_space=pltpu.SMEM),
            pl.BlockSpec((wa_count, vert_count, 1, 16, LANE), lambda s: (0, 0, s, 0, 0)),
            pl.BlockSpec((1, lat_pairs, columns), lambda s: (s, 0, 0)),
        ],
        out_specs=pl.BlockSpec((1, 2, field_count, columns), lambda s: (s, 0, 0, 0)),
        out_shape=jax.ShapeDtypeStruct((slot_count, 2, field_count, columns), jnp.float32),
        scratch_shapes=[pltpu.VMEM((lat_pairs, 4 * LANE), jnp.bfloat16)],
        compiler_params=pltpu.CompilerParams(vmem_limit_bytes=48 * 2**20),
        name="legendre",
    )(first_count, shaped, legendre)


def body(grid_values, row_length, pair_order, legendre):
    wa_count = lax.axis_size("wa")
    vert_count = lax.axis_size("vert")
    device_total = wa_count * vert_count
    order = jnp.stack([pair_order, TRUNC - pair_order], axis=1).reshape(-1)
    sent = fourier_all(grid_values, row_length, order, device_total)
    received = lax.all_to_all(sent, ("wa", "vert"), split_axis=0, concat_axis=0, tiled=True)
    slot_count = legendre.shape[0]
    owner_idx = lax.axis_index("wa") * vert_count + lax.axis_index("vert")
    local_pairs = lax.dynamic_slice_in_dim(pair_order, owner_idx * slot_count, slot_count)
    return legendre_all(received, legendre, local_pairs, wa_count, vert_count)


def solution(mesh):
    placed = (P("wa", "vert", None), P("wa"), P(), P(("wa", "vert"), None, None))
    return jax.shard_map(
        body,
        mesh=mesh,
        in_specs=placed,
        out_specs=P(("wa", "vert"), None, None, None),
        check_vma=False,
    )
```

time: 1480 us -> 113 us (0.08)
  other arithmetic: 901 us -> 2.2 us
  local copies, waits for them, and re-layouts: 383 us -> 10.8 us
  matrix products: 71.7 us -> 0 us
  waiting for transfers between devices: 91.8 us -> 25.9 us
  Pallas kernels: 0 us -> 61.5 us
    another operation x49 -> x1, other arithmetic: 558 us -> 0.01 us  [body(): order = jnp.stack([pair_order, TRUNC - pair_order], axis=1).reshape(-1)]
    dot_general x17 -> x0, local copies, waits for them, and re-layouts: 192 us -> none  [the longest x16 178 us: padded_row(): jnp.dot(masked.reshape(field_count * block_total, SUB), inner_table, pref...]
    cos x16 -> x0, other arithmetic: 186 us -> none  [row_tables(): jnp.cos(outer_angle)]
    reduce_sum x17 -> x0, other arithmetic: 114 us -> none  [the longest x16 105 us: padded_row(): jnp.sum(cos_part * twist_cos - sin_part * twist_sin, axis=1) * keep_scale]
    dot_general x17 -> x0, matrix products: 71.7 us -> none  [the longest x16 62 us: padded_row(): jnp.dot(masked.reshape(field_count * block_total, SUB), inner_table, pref...]
    pallas_call x0 -> x2, Pallas kernels: none -> 61.5 us  [the longest x1 41.6 us: fourier_all(): pl.pallas_call(fourier_kernel, grid=(GROUPS,), in_specs=[smem, smem, smem...]
    ppermute x1 -> x0, waiting for transfers between devices: 56.2 us -> none  [partner_2(): lax.ppermute(value, axis, [(i, i ^ 1 << distance) for i in range(lax.axis...]
    reshape x5 -> x0, local copies, waits for them, and re-layouts: 30.2 us -> none  [the longest x2 16.4 us: body(): fourier = lax.map(padded_row, (grid_values, row_length), batch_size=2)]
  transfers between devices with their start and end apart: 2 -> 1, of which waited for: 2 -> 1; matrix products, arithmetic and copies ran while one was open for 0% -> 9% of each run, Pallas kernels for 0% -> 0%
where the time goes in v1:
time: 113 us; the launch traced here: 112 us
  Pallas kernels  61.5 us (54%)
  waiting for transfers between devices  25.9 us (23%)
  starting transfers between devices  11.5 us (10%)
  local copies, waits for them, and re-layouts  10.8 us (10%)
  other arithmetic  2.2 us (2%)
    pallas_call x1, Pallas kernels, fourier_all(): pl.pallas_call(fourier_kernel, grid=(GROUPS,), in_specs=[smem, smem, smem...  41.6 us
    all_to_all x1, waiting for transfers between devices, body(): lax.all_to_all(sent, ('wa', 'vert'), split_axis=0, concat_axis=0, tiled=T...  25.9 us
    pallas_call x1, Pallas kernels, legendre_all(): pl.pallas_call(legendre_kernel, grid=(slot_count,), in_specs=[pl.BlockSpe...  19.9 us
    all_to_all x1, starting transfers between devices, body(): lax.all_to_all(sent, ('wa', 'vert'), split_axis=0, concat_axis=0, tiled=T...  11.5 us
    unnamed x1, local copies, waits for them, and re-layouts  9.75 us
  transfers between devices with their start and end apart: 1, of which 1 were waited for; matrix products, arithmetic and copies ran while one was open for 9% of the time, Pallas kernels for 0%

profile of v1, /device:TPU:1, one launch (start us, length us, event | category | flops | bytes accessed | tf_op | source)
XLA Modules:
  0.0 112.0 jit_solution(12597895215463421030)
XLA Ops:
  0.0 0.7 stack.9
  0.7 0.7 broadcast_subtract_fusion
  1.4 0.7 convert_divide_fusion
  2.1 0.2 copy.6
  2.3 0.2 reshape_reshape.4.order_ref
  2.5 41.6 %fourier.1 = bf16[128,80,128]{2,1,0:T(8,128)(2,1)} custom-call(s32[32]{0:T(128)S(1)} %get-tuple-element.6.quarter_ref, f32[32]{0:T(128)S(1)} %get-tuple-element.5.inv_ref, f32[32]{0:T(128)S(1)} %get-tuple-element.7.scale_ref, bf16[4,8,16,5376]{3,2,1,0:T(8,128)(2,1)} %bitcast.3, s32[1280,1]{1,0:T(8,128)S(1)} %reshape_reshape.4.order_ref), custom_call_target="tpu_custom_call" | custom-call | tf_op jit(solution)/shard_map/fourier/pallas_call | solution.py:205
  44.1 11.5 %all-to-all-start = ((bf16[128,80,128]{2,1,0:T(8,128)(2,1)}), bf16[128,80,128]{2,1,0:T(8,128)(2,1)S(1)}, u32[]{:S(2)}, u32[]{:S(2)}) async-start(bf16[128,80,128]{2,1,0:T(8,128)(2,1)} %fourier.1), calls=%async_computation | async-start | bytes 5242880 | tf_op jit(solution)/shard_map/all_to_all | solution.py:312
  55.7 9.8 %copy.8.leg_ref = bf16[5,512,1281]{2,1,0:T(8,128)(2,1)} copy(bf16[5,512,1281]{1,2,0:T(8,128)(2,1)} %param.7) | data formatting | bytes 13117440 | tf_op args[3]
  65.4 0.8 dynamic-slice_subtract_fusion.first_ref
  66.2 25.9 %all-to-all-done = bf16[128,80,128]{2,1,0:T(8,128)(2,1)S(1)} async-done(((bf16[128,80,128]{2,1,0:T(8,128)(2,1)}), bf16[128,80,128]{2,1,0:T(8,128)(2,1)S(1)}, u32[]{:S(2)}, u32[]{:S(2)}) %all-to-all-start) | async-done | bytes 2621472 | tf_op jit(solution)/shard_map/all_to_all | solution.py:312
  92.1 19.9 %legendre.1 = f32[5,2,64,1281]{3,2,1,0:T(8,128)} custom-call(s32[5]{0:T(128)S(1)} %dynamic-slice_subtract_fusion.first_ref, bf16[32,4,5,16,128]{4,3,2,1,0:T(8,128)(2,1)S(1)} %bitcast.2, bf16[5,512,1281]{2,1,0:T(8,128)(2,1)} %copy.8.leg_ref), custom_call_target="tpu_custom_call" | custom-call | tf_op jit(solution)/shard_map/legendre/pallas_call | solution.py:290
  (2 shorter events, 0.0 us)
Async XLA Ops:
  44.1 48.0 %all-to-all-start = ((bf16[128,80,128]{2,1,0:T(8,128)(2,1)}), bf16[128,80,128]{2,1,0:T(8,128)(2,1)S(1)}, u32[]{:S(2)}, u32[]{:S(2)}) async-start(bf16[128,80,128]{2,1,0:T(8,128)(2,1)} %fourier.1), calls=%async_computation | async-start | bytes 5242880 | tf_op jit(solution)/shard_map/all_to_all | solution.py:312

commit v2 on v1

v2 whole, which is shorter than its diff:
```python
import functools
import math

import jax
import jax.numpy as jnp
from jax import lax
from jax.experimental import pallas as pl
from jax.experimental.pallas import tpu as pltpu
from jax.sharding import PartitionSpec as P

TRUNC = 1279
SUB = 256
LPAD = 5376
WAVES = TRUNC + 1
CLASS = WAVES // 4
CPAD = 384
LANE = 128
CHUNKS = 11
BLOCKS = 6
GROUPS = 8
SPAN = 4
ORDER = 5
STRIDE = 37
PART = 640


def sincos(turns):
    quarter = turns * 4.0
    near = jnp.floor(quarter + 0.5)
    f = quarter - near
    f2 = f * f
    h = math.pi / 2
    s = f * (h + f2 * (-(h**3) / 6 + f2 * (h**5 / 120 + f2 * (-(h**7) / 5040 + f2 * (h**9 / 362880)))))
    c = 1.0 + f2 * (
        -(h**2) / 2 + f2 * (h**4 / 24 + f2 * (-(h**6) / 720 + f2 * (h**8 / 40320 - f2 * (h**10 / 3628800))))
    )
    which = near - 4.0 * jnp.floor(near * 0.25)
    odd = (which == 1.0) | (which == 3.0)
    cos_out = jnp.where(odd, s, c)
    sin_out = jnp.where(odd, c, s)
    cos_out = jnp.where((which == 1.0) | (which == 2.0), -cos_out, cos_out)
    sin_out = jnp.where(which >= 2.0, -sin_out, sin_out)
    return cos_out, sin_out


def turns_of(product, n_float, inv_n):
    return (product - jnp.floor(product * inv_n) * n_float) * inv_n


def iota_f(shape, dim):
    return lax.broadcasted_iota(jnp.int32, shape, dim).astype(jnp.float32)


def fold_kernel(length_ref, grid_ref, even_ref, rest_ref, twiddle):
    g = pl.program_id(0)

    @pl.when(g == 0)
    def _():
        def eight_rows(block, carry):
            sub = lax.broadcasted_iota(jnp.int32, (8, LANE), 0)
            n8 = jnp.zeros((8, LANE), jnp.int32)
            for e in range(8):
                n8 = jnp.where(sub == e, length_ref[block * 8 + e] // 4, n8)
            inv8 = 0.25 / n8.astype(jnp.float32)
            for j in range(CHUNKS):
                k = lax.broadcasted_iota(jnp.int32, (8, LANE), 1) + j * LANE
                c1, s1 = sincos(k.astype(jnp.float32) * inv8)
                c2 = c1 * c1 - s1 * s1
                s2 = 2.0 * c1 * s1
                c3 = c2 * c1 - s2 * s1
                s3 = s2 * c1 + c2 * s1
                for which, v in enumerate((c1, s1, c2, s2, c3, s3)):
                    for e in range(8):
                        twiddle[block * 8 + e, which : which + 1, j * LANE : (j + 1) * LANE] = v[e : e + 1]
            return carry

        lax.fori_loop(0, twiddle.shape[0] // 8, eight_rows, 0)

    lane = lax.broadcasted_iota(jnp.int32, (16, LANE), 1)
    zero = jnp.zeros((16, LANE), jnp.bfloat16)

    def one_row(t, carry):
        row = t * GROUPS + g
        n = length_ref[row] // 4
        starts = []
        for part in range(4):
            start = n * part
            whole = start // LANE
            shift = start - whole * LANE
            starts.append((whole, shift, lax.rem(LANE - shift, LANE)))

        def piece(part, j):
            whole, shift, back = starts[part]
            at = pl.multiple_of((whole + j) * LANE, LANE)
            value = grid_ref[t, 0, :, pl.ds(at, LANE)].astype(jnp.float32)
            return pltpu.roll(value, back, 1) if part else value

        held = [piece(part, 0) for part in range(4)]
        for j in range(CHUNKS):
            inside = lane + j * LANE < n
            quarter = []
            for part in range(4):
                value = held[part]
                following = piece(part, j + 1) if part or j + 1 < CHUNKS else None
                if part:
                    value = jnp.where(lane < LANE - starts[part][1], value, following)
                held[part] = following
                quarter.append(jnp.where(inside, value, 0.0))
            c1, s1, c2, s2, c3, s3 = (
                twiddle[row, which : which + 1, j * LANE : (j + 1) * LANE] for which in range(6)
            )
            qa, qb, qc, qd = quarter
            even = qa + qc
            even_other = qb + qd
            re = qa - qc
            im = qd - qb
            h2 = even - even_other
            q = j // 2
            at = (j % 2) * LANE
            even_ref[t, 0, q * 16 : q * 16 + 16, at : at + LANE] = (even + even_other).astype(jnp.bfloat16)
            values = (
                (re * c1 + im * s1, im * c1 - re * s1),
                (h2 * c2, -(h2 * s2)),
                (re * c3 - im * s3, -(im * c3 + re * s3)),
            )
            for r, (zr, zi) in enumerate(values):
                top = (r * BLOCKS + q) * 16
                rest_ref[t, 0, top : top + 16, at : at + LANE] = zr.astype(jnp.bfloat16)
                rest_ref[t, 0, top : top + 16, SUB + at : SUB + at + LANE] = zi.astype(jnp.bfloat16)
        for j in range(CHUNKS, 2 * BLOCKS):
            q = j // 2
            at = (j % 2) * LANE
            even_ref[t, 0, q * 16 : q * 16 + 16, at : at + LANE] = zero
            for r in range(3):
                top = (r * BLOCKS + q) * 16
                rest_ref[t, 0, top : top + 16, at : at + LANE] = zero
                rest_ref[t, 0, top : top + 16, SUB + at : SUB + at + LANE] = zero
        return carry

    lax.fori_loop(0, SPAN, one_row, 0)


def fold_all(grid_values, row_length):
    row_total, field_count, points = grid_values.shape
    return pl.pallas_call(
        fold_kernel,
        grid=(GROUPS,),
        in_specs=[
            pl.BlockSpec(memory_space=pltpu.SMEM),
            pl.BlockSpec((SPAN, 1, field_count, points), lambda g: (0, g, 0, 0)),
        ],
        out_specs=[
            pl.BlockSpec((SPAN, 1, BLOCKS * 16, SUB), lambda g: (0, g, 0, 0)),
            pl.BlockSpec((SPAN, 1, 3 * BLOCKS * 16, 2 * SUB), lambda g: (0, g, 0, 0)),
        ],
        out_shape=[
            jax.ShapeDtypeStruct((SPAN, GROUPS, BLOCKS * 16, SUB), jnp.bfloat16),
            jax.ShapeDtypeStruct((SPAN, GROUPS, 3 * BLOCKS * 16, 2 * SUB), jnp.bfloat16),
        ],
        scratch_shapes=[pltpu.VMEM((row_total, 8, CHUNKS * LANE), jnp.float32)],
        compiler_params=pltpu.CompilerParams(vmem_limit_bytes=60 * 2**20),
        name="fold",
    )(row_length, grid_values.reshape(SPAN, GROUPS, field_count, points))


def fourier_kernel(
    length_ref,
    order_ref,
    even_ref,
    rest_ref,
    out_ref,
    rhs,
    small,
    onehot,
    rows,
    spread,
    sending,
    landing,
    local_sem,
    send_sem,
    recv_sem,
):
    g = pl.program_id(0)
    vert_count = lax.axis_size("vert")
    total = lax.axis_size("wa") * vert_count
    me = lax.axis_index("wa") * vert_count + lax.axis_index("vert")
    dest_rows = WAVES * GROUPS // total
    per_dest = WAVES // total

    def place(device):
        return (device // vert_count, lax.rem(device, vert_count))

    @pl.when(g == 0)
    def _():
        barrier = pltpu.get_barrier_semaphore()

        def greet(i, carry):
            other = lax.rem(me + i, total)
            pl.semaphore_signal(barrier, 1, device_id=place(other), device_id_type=pl.DeviceIdType.MESH)
            return carry

        lax.fori_loop(1, total, greet, 0)
        for c in range(per_dest):
            pair = order_ref[:, c // 2 : c // 2 + 1]
            target = TRUNC - pair if c % 2 else pair
            for r in range(4):
                wave = lax.broadcasted_iota(jnp.int32, (total, CPAD), 1) * 4 + r
                wave = jnp.where(wave < WAVES, wave, -1)
                onehot[c * total : (c + 1) * total, r * CPAD : (r + 1) * CPAD] = (
                    (wave == target).astype(jnp.float32).astype(jnp.bfloat16)
                )

    def prepare(t):
        slot = t % 2
        n = jnp.full((8, CPAD), length_ref[t * GROUPS + g] // 4, jnp.int32)
        n_float = n.astype(jnp.float32)
        inv_n = 1.0 / n_float
        u = iota_f((8, CPAD), 1)
        low = iota_f((8, CPAD), 0)
        mixed = jnp.where(low == 0.0, 8.0, jnp.where(low == 1.0, 128.0, 256.0 * (low - 1.0)))
        cb, sb = sincos(turns_of(low * u, n_float, inv_n))
        ct, st = sincos(turns_of(low * 16.0 * u, n_float, inv_n))
        cm, sm = sincos(turns_of(mixed * u, n_float, inv_n))
        small[slot, 0, :8] = ct
        small[slot, 1, :8] = st
        small[slot, 0, 16:] = cm
        small[slot, 1, 16:] = sm
        c8, s8 = small[slot, 0, 16:17, :], small[slot, 1, 16:17, :]
        c128, s128 = small[slot, 0, 17:18, :], small[slot, 1, 17:18, :]
        small[slot, 0, 8:16] = ct * c128 - st * s128
        small[slot, 1, 8:16] = st * c128 + ct * s128
        base = ((cb, sb), (cb * c8 - sb * s8, sb * c8 + cb * s8))
        for a in range(16):
            ca = small[slot, 0, a : a + 1, :]
            sa = small[slot, 1, a : a + 1, :]
            c = jnp.concatenate([x * ca - y * sa for x, y in base], axis=0)
            s = jnp.concatenate([y * ca + x * sa for x, y in base], axis=0)
            c16 = c.astype(jnp.bfloat16)
            s16 = s.astype(jnp.bfloat16)
            rhs[slot, a * 16 : a * 16 + 16, :CPAD] = c16
            rhs[slot, a * 16 : a * 16 + 16, CPAD:] = -s16
            rhs[slot, SUB + a * 16 : SUB + a * 16 + 16, :CPAD] = s16
            rhs[slot, SUB + a * 16 : SUB + a * 16 + 16, CPAD:] = c16

    paired = (g == 1) | (g == 3) | (g == 6)

    def finish(t, sums):
        slot = t % 2
        length = jnp.full((1, CPAD), length_ref[t * GROUPS + g], jnp.int32)
        scale = 1.0 / jnp.sqrt(length.astype(jnp.float32))
        column = lax.broadcasted_iota(jnp.int32, (1, CPAD), 1)
        lane_top = pl.multiple_of(jnp.where(paired, LANE, 0) + t * 32, 32)
        for r in range(4):
            part_sum, first = (sums[0], 0) if r == 0 else (sums[1], (r - 1) * 96)
            real = part_sum[first : first + 16, :CPAD]
            imag = part_sum[first : first + 16, CPAD:]
            for q in range(1, BLOCKS):
                top = first + q * 16
                pr = part_sum[top : top + 16, :CPAD]
                pi = part_sum[top : top + 16, CPAD:]
                c = small[slot, 0, 17 + q : 18 + q, :]
                s = small[slot, 1, 17 + q : 18 + q, :]
                real = real + (pr * c + pi * s)
                imag = imag + (pi * c - pr * s)
            wave = column * 4 + r
            keep = jnp.where((wave * 2 <= length - 1) & (column < CLASS), scale, 0.0)
            rows[pl.ds(lane_top, 16), r * CPAD : (r + 1) * CPAD] = (real * keep).astype(jnp.bfloat16)
            rows[pl.ds(lane_top + 16, 16), r * CPAD : (r + 1) * CPAD] = (imag * keep).astype(jnp.bfloat16)

    prepare(0)
    for t in range(SPAN):
        sums = (
            jnp.dot(even_ref[t, 0], rhs[t % 2, :SUB], preferred_element_type=jnp.float32),
            jnp.dot(rest_ref[t, 0], rhs[t % 2], preferred_element_type=jnp.float32),
        )
        if t + 1 < SPAN:
            prepare(t + 1)
        finish(t, sums)

    def order(count):
        for c0 in range(0, per_dest, ORDER):
            picked = lax.dot_general(
                onehot[c0 * total : (c0 + ORDER) * total, :],
                rows[: count * LANE, :],
                (((1,), (1,)), ((), ())),
                preferred_element_type=jnp.float32,
            )
            for c in range(ORDER):
                for e in range(count):
                    at = (g - count + 1 + e) * per_dest + c0 + c
                    spread[pl.ds(at, total, stride=dest_rows), :] = picked[
                        c * total : (c + 1) * total, e * LANE : (e + 1) * LANE
                    ]

    pl.when(paired)(lambda: order(2))
    pl.when((g == 4) | (g == 7))(lambda: order(1))

    @pl.when(paired | (g == 4) | (g == 7))
    def _():
        tile = (5 * (g + 1)) // 8 - 1

        def convert(d, carry):
            sending[tile, d] = spread[pl.ds(pl.multiple_of(d * dest_rows + tile * 16, 16), 16), :].astype(jnp.bfloat16)
            return carry

        lax.fori_loop(0, total, convert, 0, unroll=8)

        @pl.when(g == 1)
        def _():
            pl.semaphore_wait(pltpu.get_barrier_semaphore(), total - 1)

        pltpu.make_async_copy(sending.at[tile, me], landing.at[tile, me], local_sem.at[tile]).start()

        def send(i, carry):
            other = lax.rem(me + i * STRIDE, total)
            pltpu.make_async_remote_copy(
                sending.at[tile, other],
                landing.at[tile, me],
                send_sem.at[tile],
                recv_sem.at[tile],
                device_id=place(other),
                device_id_type=pl.DeviceIdType.MESH,
            ).start()
            return carry

        lax.fori_loop(1, total, send, 0)

    @pl.when(g == GROUPS - 1)
    def _():
        tiles = out_ref.shape[0]
        others = pl.ds(0, total - 1)
        for tile in range(tiles):
            pltpu.make_async_copy(sending.at[tile, me], landing.at[tile, me], local_sem.at[tile]).wait()
            pltpu.make_async_copy(sending.at[tile, others], landing.at[tile, others], recv_sem.at[tile]).wait()
            pltpu.make_async_copy(landing.at[tile], out_ref.at[tile], local_sem.at[tile]).start()
        for tile in range(tiles):
            pltpu.make_async_copy(sending.at[tile, others], landing.at[tile, others], send_sem.at[tile]).wait()
            pltpu.make_async_copy(landing.at[tile], out_ref.at[tile], local_sem.at[tile]).wait()


def fourier_all(row_length, pair_order, even, rest, device_total):
    tiles = WAVES * GROUPS // device_total // 16
    return pl.pallas_call(
        fourier_kernel,
        grid=(GROUPS,),
        in_specs=[
            pl.BlockSpec(memory_space=pltpu.SMEM),
            pl.BlockSpec((device_total, pair_order.shape[0] // device_total), lambda g: (0, 0)),
            pl.BlockSpec((SPAN, 1) + even.shape[2:], lambda g: (0, g, 0, 0)),
            pl.BlockSpec((SPAN, 1) + rest.shape[2:], lambda g: (0, g, 0, 0)),
        ],
        out_specs=pl.BlockSpec(memory_space=pl.ANY),
        out_shape=jax.ShapeDtypeStruct((tiles, device_total, 16, LANE), jnp.bfloat16),
        scratch_shapes=[
            pltpu.VMEM((2, 2 * SUB, 2 * CPAD), jnp.bfloat16),
            pltpu.VMEM((2, 2, 24, CPAD), jnp.float32),
            pltpu.VMEM((WAVES, 4 * CPAD), jnp.bfloat16),
            pltpu.VMEM((2 * LANE, 4 * CPAD), jnp.bfloat16),
            pltpu.VMEM((WAVES * GROUPS, LANE), jnp.float32),
            pltpu.VMEM((tiles, device_total, 16, LANE), jnp.bfloat16),
            pltpu.VMEM((tiles, device_total, 16, LANE), jnp.bfloat16),
            pltpu.SemaphoreType.DMA((tiles,)),
            pltpu.SemaphoreType.DMA((tiles,)),
            pltpu.SemaphoreType.DMA((tiles,)),
        ],
        compiler_params=pltpu.CompilerParams(
            vmem_limit_bytes=60 * 2**20, collective_id=0, has_side_effects=True
        ),
        name="fourier",
    )(row_length, pair_order.reshape(device_total, -1), even, rest)


def legendre_kernel(pair_ref, recv_ref, leg_ref, out_ref, operand, loose):
    slot = pl.program_id(0)
    owner = lax.axis_index("wa") * lax.axis_size("vert") + lax.axis_index("vert")

    @pl.when(slot == 0)
    def _():
        lane = lax.broadcasted_iota(jnp.int32, (8, LANE), 1)
        odd32 = (lane // 32) % 2 == 1
        high64 = lane >= 64
        per_dest = loose.shape[2] // GROUPS
        half = recv_ref.shape[1] // 2

        def regroup(tiles):
            a, b, c, d = tiles
            ab0 = jnp.where(odd32, pltpu.roll(b, 32, 1), a)
            ab1 = jnp.where(odd32, b, pltpu.roll(a, 96, 1))
            cd0 = jnp.where(odd32, pltpu.roll(d, 32, 1), c)
            cd1 = jnp.where(odd32, d, pltpu.roll(c, 96, 1))
            return (
                jnp.where(high64, pltpu.roll(cd0, 64, 1), ab0),
                jnp.where(high64, pltpu.roll(cd1, 64, 1), ab1),
                jnp.where(high64, cd0, pltpu.roll(ab0, 64, 1)),
                jnp.where(high64, cd1, pltpu.roll(ab1, 64, 1)),
            )

        def pair(w, carry):
            for side in range(2):
                for v in range(4):
                    for tile in range(recv_ref.shape[0]):
                        loose[side, v, tile * 16 : tile * 16 + 16, :] = recv_ref[tile, side * half + w, v].astype(
                            jnp.float32
                        )
            for col in range(per_dest):
                north, south = (
                    regroup([loose[side, v, pl.ds(col, 8, stride=per_dest), :] for v in range(4)]) for side in range(2)
                )
                for t in range(0, 4, 2):
                    top = pl.multiple_of(w * 32 + t * 8, 16)
                    sums = [north[t + e] + south[t + e] for e in range(2)]
                    differences = [north[t + e] - south[t + e] for e in range(2)]
                    for kind, both in enumerate((sums, differences)):
                        at = ((col % 2) * 2 + kind) * LANE
                        operand[col // 2, pl.ds(top, 16), at : at + LANE] = jnp.concatenate(both, axis=0).astype(
                            jnp.bfloat16
                        )
            return carry

        lax.fori_loop(0, half, pair, 0)

    first_count = WAVES - pair_ref[owner * pl.num_programs(0) + slot]
    columns = leg_ref.shape[1]
    whole = columns // LANE * LANE

    def choose(product, top, out_lanes):
        height = product.shape[0]
        column = lax.broadcasted_iota(jnp.int32, (height, LANE), 0) + top
        in_first = column < first_count
        degree = jnp.where(in_first, column, column - first_count)
        even = degree % 2 == 0
        s0, a0, s1, a1 = (product[:, k * LANE : (k + 1) * LANE] for k in range(4))
        chosen = jnp.where(in_first, jnp.where(even, s0, a0), jnp.where(even, s1, a1))
        turned = chosen.T
        for v in range(4):
            for i in range(2):
                at = v * 32 + i * 16
                out_ref[0, i, v * 16 : v * 16 + 16, out_lanes] = turned[at : at + 16]

    for start in range(0, whole, PART):
        product = jnp.dot(
            leg_ref[0, start : start + PART, :], operand[slot], preferred_element_type=jnp.float32
        )
        for top in range(0, PART, LANE):
            choose(product[top : top + LANE], start + top, slice(start + top, start + top + LANE))
    last = leg_ref[0, whole:columns, :]
    product = jnp.dot(
        jnp.broadcast_to(last, (16, last.shape[1])), operand[slot], preferred_element_type=jnp.float32
    )
    column = jnp.zeros((16, LANE), jnp.int32) + whole
    in_first = column < first_count
    degree = jnp.where(in_first, column, column - first_count)
    even = degree % 2 == 0
    s0, a0, s1, a1 = (product[:, k * LANE : (k + 1) * LANE] for k in range(4))
    chosen = jnp.where(in_first, jnp.where(even, s0, a0), jnp.where(even, s1, a1))
    turned = jnp.broadcast_to(chosen[:1], (LANE, LANE)).T
    for v in range(4):
        for i in range(2):
            at = v * 32 + i * 16
            out_ref[0, i, v * 16 : v * 16 + 16, whole:columns] = turned[at : at + 16, : columns - whole]


def legendre_all(received, legendre, pair_order, wa_count, vert_count):
    slot_count, lat_pairs, columns = legendre.shape
    field_count = 16 * vert_count
    tiles = received.shape[0]
    turned = jnp.swapaxes(legendre, 1, 2)
    shaped = received.reshape(tiles, wa_count, vert_count, 16, LANE)
    return pl.pallas_call(
        legendre_kernel,
        grid=(slot_count,),
        in_specs=[
            pl.BlockSpec(memory_space=pltpu.SMEM),
            pl.BlockSpec(shaped.shape, lambda s: (0, 0, 0, 0, 0)),
            pl.BlockSpec((1, columns, lat_pairs), lambda s: (s, 0, 0)),
        ],
        out_specs=pl.BlockSpec((1, 2, field_count, columns), lambda s: (s, 0, 0, 0)),
        out_shape=jax.ShapeDtypeStruct((slot_count, 2, field_count, columns), jnp.float32),
        scratch_shapes=[
            pltpu.VMEM((slot_count, lat_pairs, 4 * LANE), jnp.bfloat16),
            pltpu.VMEM((2, vert_count, tiles * 16, LANE), jnp.float32),
        ],
        compiler_params=pltpu.CompilerParams(vmem_limit_bytes=60 * 2**20),
        name="legendre",
    )(pair_order, shaped, turned)


def body(grid_values, row_length, pair_order, legendre):
    wa_count = lax.axis_size("wa")
    vert_count = lax.axis_size("vert")
    device_total = wa_count * vert_count
    even, rest = fold_all(grid_values, row_length)
    received = fourier_all(row_length, pair_order, even, rest, device_total)
    return legendre_all(received, legendre, pair_order, wa_count, vert_count)


def solution(mesh):
    placed = (P("wa", "vert", None), P("wa"), P(), P(("wa", "vert"), None, None))
    return jax.shard_map(
        body,
        mesh=mesh,
        in_specs=placed,
        out_specs=P(("wa", "vert"), None, None, None),
        check_vma=False,
    )
```

time: 113 us -> 86.3 us (0.76)
  waiting for transfers between devices: 25.9 us -> 0 us
  Pallas kernels: 61.5 us -> 84.2 us
  starting transfers between devices: 11.5 us -> 0 us
  local copies, waits for them, and re-layouts: 10.8 us -> 1.52 us
  other arithmetic: 2.2 us -> 0 us
    pallas_call x1 -> x2, Pallas kernels: 41.6 us -> 71.5 us  [the longest x1 58.6 us: fourier_all(): pl.pallas_call(fourier_kernel, grid=(GROUPS,), in_specs=[pl.BlockSpec(mem...]
    all_to_all x1 -> x0, waiting for transfers between devices: 25.9 us -> none  [body(): lax.all_to_all(sent, ('wa', 'vert'), split_axis=0, concat_axis=0, tiled=T...]
    all_to_all x1 -> x0, starting transfers between devices: 11.5 us -> none  [body(): lax.all_to_all(sent, ('wa', 'vert'), split_axis=0, concat_axis=0, tiled=T...]
    unnamed x1 -> x0, local copies, waits for them, and re-layouts: 9.75 us -> none
    pallas_call x1, Pallas kernels: 19.9 us -> 12.8 us  [legendre_all(): pl.pallas_call(legendre_kernel, grid=(slot_count,), in_specs=[pl.BlockSpe...]
    reshape x0 -> x1, local copies, waits for them, and re-layouts: none -> 1.52 us  [fourier_all(): pair_order.reshape(device_total, -1)]
    sub x2 -> x0, other arithmetic: 1.45 us -> none  [the longest x1 0.76 us: legendre_all(): first_count = (WAVES - local_pairs).astype(jnp.int32)]
  transfers between devices with their start and end apart: 1 -> 0, of which waited for: 1 -> 0; matrix products, arithmetic and copies ran while one was open for 9% -> 0% of each run, Pallas kernels for 0% -> 0%
where the time goes in v2:
time: 86.3 us; the launch traced here: 85.8 us
  Pallas kernels  84.2 us (98%)
  local copies, waits for them, and re-layouts  1.52 us (2%)
    pallas_call x1, Pallas kernels, fourier_all(): pl.pallas_call(fourier_kernel, grid=(GROUPS,), in_specs=[pl.BlockSpec(mem...  58.6 us
    pallas_call x1, Pallas kernels, fold_all(): pl.pallas_call(fold_kernel, grid=(GROUPS,), in_specs=[pl.BlockSpec(memory...  12.8 us
    pallas_call x1, Pallas kernels, legendre_all(): pl.pallas_call(legendre_kernel, grid=(slot_count,), in_specs=[pl.BlockSpe...  12.8 us

profile of v2, /device:TPU:1, one launch (start us, length us, event | category | flops | bytes accessed | tf_op | source)
XLA Modules:
  0.0 85.8 jit_solution(7358221512187588254)
XLA Ops:
  0.0 1.5 %reshape.9.order_ref = s32[128,5]{1,0:T(8,128)} reshape(s32[640]{0:T(1024)} %pair_ref.1) | data formatting | bytes 5120 | tf_op jit(solution)/shard_map/reshape | solution.py:370
  1.5 12.8 %fold.1 = (bf16[4,8,96,256]{3,2,1,0:T(8,128)(2,1)}, bf16[4,8,288,512]{3,2,1,0:T(8,128)(2,1)}) custom-call(s32[32]{0:T(128)} %length_ref.3, bf16[4,8,16,5376]{3,2,1,0:T(8,128)(2,1)} %bitcast.5), custom_call_target="tpu_custom_call" | custom-call | tf_op jit(solution)/shard_map/fold/pallas_call | solution.py:145
  14.4 58.6 %fourier.1 = bf16[5,128,16,128]{3,2,1,0:T(8,128)(2,1)} custom-call(s32[32]{0:T(128)} %length_ref.3, s32[128,5]{1,0:T(8,128)} %reshape.9.order_ref, bf16[4,8,96,256]{3,2,1,0:T(8,128)(2,1)} %get-tuple-element.7.even_ref, bf16[4,8,288,512]{3,2,1,0:T(8,128)(2,1)} %get-tuple-element.8.rest_ref), custom_call_target="tpu_custom_call" | custom-call | tf_op jit(solution)/shard_map/fourier/pallas_call | solution.py:343
  73.0 12.8 %legendre.1 = f32[5,2,64,1281]{3,2,1,0:T(8,128)} custom-call(s32[640]{0:T(1024)} %pair_ref.1, bf16[5,32,4,16,128]{4,3,2,1,0:T(8,128)(2,1)} %bitcast.3, bf16[5,1281,512]{2,1,0:T(8,128)(2,1)} %bitcast.4), custom_call_target="tpu_custom_call" | custom-call | tf_op jit(solution)/shard_map/legendre/pallas_call | solution.py:469

commit v3 on v2

--- a/solution.py
+++ b/solution.py
@@ -20,7 +20,7 @@
 GROUPS = 8
 SPAN = 4
 ORDER = 5
-STRIDE = 37
+STRIDE = 13
 PART = 640
 
 
@@ -158,7 +158,7 @@
             jax.ShapeDtypeStruct((SPAN, GROUPS, 3 * BLOCKS * 16, 2 * SUB), jnp.bfloat16),
         ],
         scratch_shapes=[pltpu.VMEM((row_total, 8, CHUNKS * LANE), jnp.float32)],
-        compiler_params=pltpu.CompilerParams(vmem_limit_bytes=60 * 2**20),
+        compiler_params=pltpu.CompilerParams(vmem_limit_bytes=16 * 2**20),
         name="fold",
     )(row_length, grid_values.reshape(SPAN, GROUPS, field_count, points))
 
@@ -311,19 +311,29 @@
 
         pltpu.make_async_copy(sending.at[tile, me], landing.at[tile, me], local_sem.at[tile]).start()
 
-        def send(i, carry):
-            other = lax.rem(me + i * STRIDE, total)
+        wa_count = lax.axis_size("wa")
+        wa, vert = lax.axis_index("wa"), lax.axis_index("vert")
+
+        def send(to_wa, to_vert):
             pltpu.make_async_remote_copy(
-                sending.at[tile, other],
+                sending.at[tile, to_wa * vert_count + to_vert],
                 landing.at[tile, me],
                 send_sem.at[tile],
                 recv_sem.at[tile],
-                device_id=place(other),
+                device_id=(to_wa, to_vert),
                 device_id_type=pl.DeviceIdType.MESH,
             ).start()
+
+        for i in range(1, vert_count):
+            send(wa, lax.rem(vert + i, vert_count))
+
+        def spoke(i, carry):
+            to_wa = lax.rem(wa + i * STRIDE, wa_count)
+            for to_vert in range(vert_count):
+                send(to_wa, to_vert)
             return carry
 
-        lax.fori_loop(1, total, send, 0)
+        lax.fori_loop(1, wa_count, spoke, 0)
 
     @pl.when(g == GROUPS - 1)
     def _():
@@ -364,7 +374,7 @@
             pltpu.SemaphoreType.DMA((tiles,)),
         ],
         compiler_params=pltpu.CompilerParams(
-            vmem_limit_bytes=60 * 2**20, collective_id=0, has_side_effects=True
+            vmem_limit_bytes=34 * 2**20, collective_id=0, has_side_effects=True
         ),
         name="fourier",
     )(row_length, pair_order.reshape(device_total, -1), even, rest)
@@ -480,7 +490,7 @@
             pltpu.VMEM((slot_count, lat_pairs, 4 * LANE), jnp.bfloat16),
             pltpu.VMEM((2, vert_count, tiles * 16, LANE), jnp.float32),
         ],
-        compiler_params=pltpu.CompilerParams(vmem_limit_bytes=60 * 2**20),
+        compiler_params=pltpu.CompilerParams(vmem_limit_bytes=24 * 2**20),
         name="legendre",
     )(pair_order, shaped, turned)
 

time: 86.3 us -> 75.7 us (0.88)
  Pallas kernels: 84.2 us -> 71.3 us
  local copies, waits for them, and re-layouts: 1.52 us -> 4.13 us
    pallas_call x1, Pallas kernels: 58.6 us -> 51 us  [fourier_all(): pl.pallas_call(fourier_kernel, grid=(GROUPS,), in_specs=[pl.BlockSpec(mem...]
    unnamed x0 -> x12, local copies, waits for them, and re-layouts: none -> 3.24 us
    pallas_call x1, Pallas kernels: 12.8 us -> 10.1 us  [legendre_all(): pl.pallas_call(legendre_kernel, grid=(slot_count,), in_specs=[pl.BlockSpe...]
    pallas_call x1, Pallas kernels: 12.8 us -> 10.2 us  [fold_all(): pl.pallas_call(fold_kernel, grid=(GROUPS,), in_specs=[pl.BlockSpec(memory...]
where the time goes in v3:
time: 75.7 us; the launch traced here: 75.5 us
  Pallas kernels  71.3 us (94%)
  local copies, waits for them, and re-layouts  4.13 us (5%)
    pallas_call x1, Pallas kernels, fourier_all(): pl.pallas_call(fourier_kernel, grid=(GROUPS,), in_specs=[pl.BlockSpec(mem...  51 us
    pallas_call x1, Pallas kernels, fold_all(): pl.pallas_call(fold_kernel, grid=(GROUPS,), in_specs=[pl.BlockSpec(memory...  10.2 us
    pallas_call x1, Pallas kernels, legendre_all(): pl.pallas_call(legendre_kernel, grid=(slot_count,), in_specs=[pl.BlockSpe...  10.1 us
    unnamed x12, local copies, waits for them, and re-layouts  3.24 us

profile of v3, /device:TPU:1, one launch (start us, length us, event | category | flops | bytes accessed | tf_op | source)
XLA Modules:
  0.0 75.5 jit_solution(10614984713640908874)
XLA Ops:
  0.0 0.0 copy-start.3
  0.0 0.9 %reshape.9.order_ref = s32[128,5]{1,0:T(8,128)S(1)} reshape(s32[640]{0:T(1024)} %pair_ref.1) | data formatting | bytes 5120 | tf_op jit(solution)/shard_map/reshape | solution.py:380
  0.9 0.0 copy-start
  0.9 2.6 %copy-done = bf16[32,16,5376]{2,1,0:T(8,128)(2,1)S(1)} copy-done((bf16[32,16,5376]{2,1,0:T(8,128)(2,1)S(1)}, bf16[32,16,5376]{2,1,0:T(8,128)(2,1)}, u32[]{:S(2)}) %copy-start) | copy-done | bytes 5505048
  3.5 0.0 copy-start.2
  3.5 0.7 copy-done.2
  4.1 0.0 slice-start
  4.1 10.2 %fold.1 = (bf16[4,8,96,256]{3,2,1,0:T(8,128)(2,1)S(1)}, bf16[4,8,288,512]{3,2,1,0:T(8,128)(2,1)S(1)}) custom-call(s32[32]{0:T(128)S(1)} %copy-done.2, bf16[4,8,16,5376]{3,2,1,0:T(8,128)(2,1)S(1)} %bitcast.7), custom_call_target="tpu_custom_call" | custom-call | tf_op jit(solution)/shard_map/fold/pallas_call | solution.py:145
  14.3 0.0 copy-done.3
  14.3 0.0 slice-start.1
  14.3 0.0 copy-start.1
  14.3 51.0 %fourier.1 = bf16[5,128,16,128]{3,2,1,0:T(8,128)(2,1)S(1)} custom-call(s32[32]{0:T(128)S(1)} %copy-done.3, s32[128,5]{1,0:T(8,128)S(1)} %reshape.9.order_ref, bf16[4,8,96,256]{3,2,1,0:T(8,128)(2,1)S(1)} %get-tuple-element.7.even_ref, bf16[4,8,288,512]{3,2,1,0:T(8,128)(2,1)S(1)} %get-tuple-element.8.rest_ref), custom_call_target="tpu_custom_call" | custom-call | tf_op jit(solution)/shard_map/fourier/pallas_call | solution.py:353
  65.4 0.0 slice-done
  65.4 0.0 slice-done.1
  65.4 0.0 copy-done.1
  65.4 10.1 %legendre.1 = f32[5,2,64,1281]{3,2,1,0:T(8,128)} custom-call(s32[640]{0:T(1024)S(1)} %copy-done.1, bf16[5,32,4,16,128]{4,3,2,1,0:T(8,128)(2,1)S(1)} %bitcast.3, bf16[5,1281,512]{2,1,0:T(8,128)(2,1)S(1)} %bitcast.6), custom_call_target="tpu_custom_call" | custom-call | tf_op jit(solution)/shard_map/legendre/pallas_call | solution.py:479
  (1 shorter events, 0.0 us)
Async XLA Ops:
  0.0 14.3 %copy-start.3 = (s32[32]{0:T(128)S(1)}, s32[32]{0:T(128)}, u32[]{:S(2)}) copy-start(s32[32]{0:T(128)} %length_ref.3) | copy-start | bytes 388
  0.9 2.6 %copy-start = (bf16[32,16,5376]{2,1,0:T(8,128)(2,1)S(1)}, bf16[32,16,5376]{2,1,0:T(8,128)(2,1)}, u32[]{:S(2)}) copy-start(bf16[32,16,5376]{2,1,0:T(8,128)(2,1)} %param.4) | copy-start | bytes 16515076
  3.5 0.7 copy-start.2
  4.1 61.2 %slice-start = ((s8[6594560]{0:T(1024)(128)(4,1)}), s8[4194304]{0:T(1024)(128)(4,1)S(1)}, s32[]{:S(2)}) async-start(s8[6594560]{0:T(1024)(128)(4,1)} %bitcast.4), calls=%async_computation | async-start | bytes 8388608
  14.3 51.1 %slice-start.1 = ((s8[6594560]{0:T(1024)(128)(4,1)}), s8[2400256]{0:T(1024)(128)(4,1)S(1)}, s32[]{:S(2)}) async-start(s8[6594560]{0:T(1024)(128)(4,1)} %bitcast.4), calls=%async_computation.1 | async-start | bytes 4800512
  14.3 51.1 %copy-start.1 = (s32[640]{0:T(1024)S(1)}, s32[640]{0:T(1024)}, u32[]{:S(2)}) copy-start(s32[640]{0:T(1024)} %pair_ref.1) | copy-start | bytes 7684

commit v4 on v3

--- a/solution.py
+++ b/solution.py
@@ -52,34 +52,32 @@
 
 
 def fold_kernel(length_ref, grid_ref, even_ref, rest_ref, twiddle):
-    g = pl.program_id(0)
-
-    @pl.when(g == 0)
-    def _():
-        def eight_rows(block, carry):
-            sub = lax.broadcasted_iota(jnp.int32, (8, LANE), 0)
-            n8 = jnp.zeros((8, LANE), jnp.int32)
-            for e in range(8):
-                n8 = jnp.where(sub == e, length_ref[block * 8 + e] // 4, n8)
-            inv8 = 0.25 / n8.astype(jnp.float32)
-            for j in range(CHUNKS):
-                k = lax.broadcasted_iota(jnp.int32, (8, LANE), 1) + j * LANE
-                c1, s1 = sincos(k.astype(jnp.float32) * inv8)
-                c2 = c1 * c1 - s1 * s1
-                s2 = 2.0 * c1 * s1
-                c3 = c2 * c1 - s2 * s1
-                s3 = s2 * c1 + c2 * s1
-                for which, v in enumerate((c1, s1, c2, s2, c3, s3)):
-                    for e in range(8):
-                        twiddle[block * 8 + e, which : which + 1, j * LANE : (j + 1) * LANE] = v[e : e + 1]
-            return carry
-
-        lax.fori_loop(0, twiddle.shape[0] // 8, eight_rows, 0)
+    def eight_rows(block, carry):
+        sub = lax.broadcasted_iota(jnp.int32, (8, LANE), 0)
+        n8 = jnp.zeros((8, LANE), jnp.int32)
+        for e in range(8):
+            n8 = jnp.where(sub == e, length_ref[block * 8 + e] // 4, n8)
+        inv8 = 0.25 / n8.astype(jnp.float32)
+        for j in range(CHUNKS):
+            k = lax.broadcasted_iota(jnp.int32, (8, LANE), 1) + j * LANE
+            c1, s1 = sincos(k.astype(jnp.float32) * inv8)
+            c2 = c1 * c1 - s1 * s1
+            s2 = 2.0 * c1 * s1
+            c3 = c2 * c1 - s2 * s1
+            s3 = s2 * c1 + c2 * s1
+            inside = k < n8
+            for which, v in enumerate((c1, s1, c2, s2, c3, s3)):
+                v = jnp.where(inside, v, 0.0)
+                for e in range(8):
+                    twiddle[block * 8 + e, which : which + 1, j * LANE : (j + 1) * LANE] = v[e : e + 1]
+        return carry
+
+    lax.fori_loop(0, twiddle.shape[0] // 8, eight_rows, 0)
 
     lane = lax.broadcasted_iota(jnp.int32, (16, LANE), 1)
     zero = jnp.zeros((16, LANE), jnp.bfloat16)
 
-    def one_row(t, carry):
+    def one_row(t, g):
         row = t * GROUPS + g
         n = length_ref[row] // 4
         starts = []
@@ -92,7 +90,7 @@
         def piece(part, j):
             whole, shift, back = starts[part]
             at = pl.multiple_of((whole + j) * LANE, LANE)
-            value = grid_ref[t, 0, :, pl.ds(at, LANE)].astype(jnp.float32)
+            value = grid_ref[t, g, :, pl.ds(at, LANE)].astype(jnp.float32)
             return pltpu.roll(value, back, 1) if part else value
 
         held = [piece(part, 0) for part in range(4)]
@@ -105,7 +103,7 @@
                 if part:
                     value = jnp.where(lane < LANE - starts[part][1], value, following)
                 held[part] = following
-                quarter.append(jnp.where(inside, value, 0.0))
+                quarter.append(value)
             c1, s1, c2, s2, c3, s3 = (
                 twiddle[row, which : which + 1, j * LANE : (j + 1) * LANE] for which in range(6)
             )
@@ -117,7 +115,9 @@
             h2 = even - even_other
             q = j // 2
             at = (j % 2) * LANE
-            even_ref[t, 0, q * 16 : q * 16 + 16, at : at + LANE] = (even + even_other).astype(jnp.bfloat16)
+            even_ref[t, g, q * 16 : q * 16 + 16, at : at + LANE] = jnp.where(
+                inside, even + even_other, 0.0
+            ).astype(jnp.bfloat16)
             values = (
                 (re * c1 + im * s1, im * c1 - re * s1),
                 (h2 * c2, -(h2 * s2)),
@@ -125,34 +125,31 @@
             )
             for r, (zr, zi) in enumerate(values):
                 top = (r * BLOCKS + q) * 16
-                rest_ref[t, 0, top : top + 16, at : at + LANE] = zr.astype(jnp.bfloat16)
-                rest_ref[t, 0, top : top + 16, SUB + at : SUB + at + LANE] = zi.astype(jnp.bfloat16)
+                rest_ref[t, g, top : top + 16, at : at + LANE] = zr.astype(jnp.bfloat16)
+                rest_ref[t, g, top : top + 16, SUB + at : SUB + at + LANE] = zi.astype(jnp.bfloat16)
         for j in range(CHUNKS, 2 * BLOCKS):
             q = j // 2
             at = (j % 2) * LANE
-            even_ref[t, 0, q * 16 : q * 16 + 16, at : at + LANE] = zero
+            even_ref[t, g, q * 16 : q * 16 + 16, at : at + LANE] = zero
             for r in range(3):
                 top = (r * BLOCKS + q) * 16
-                rest_ref[t, 0, top : top + 16, at : at + LANE] = zero
-                rest_ref[t, 0, top : top + 16, SUB + at : SUB + at + LANE] = zero
+                rest_ref[t, g, top : top + 16, at : at + LANE] = zero
+                rest_ref[t, g, top : top + 16, SUB + at : SUB + at + LANE] = zero
+        return g
+
+    def one_group(g, carry):
+        lax.fori_loop(0, SPAN, one_row, g)
         return carry
 
-    lax.fori_loop(0, SPAN, one_row, 0)
+    lax.fori_loop(0, GROUPS, one_group, 0)
 
 
 def fold_all(grid_values, row_length):
     row_total, field_count, points = grid_values.shape
     return pl.pallas_call(
         fold_kernel,
-        grid=(GROUPS,),
-        in_specs=[
-            pl.BlockSpec(memory_space=pltpu.SMEM),
-            pl.BlockSpec((SPAN, 1, field_count, points), lambda g: (0, g, 0, 0)),
-        ],
-        out_specs=[
-            pl.BlockSpec((SPAN, 1, BLOCKS * 16, SUB), lambda g: (0, g, 0, 0)),
-            pl.BlockSpec((SPAN, 1, 3 * BLOCKS * 16, 2 * SUB), lambda g: (0, g, 0, 0)),
-        ],
+        in_specs=[pl.BlockSpec(memory_space=pltpu.SMEM), pl.BlockSpec(memory_space=pltpu.VMEM)],
+        out_specs=[pl.BlockSpec(memory_space=pltpu.VMEM)] * 2,
         out_shape=[
             jax.ShapeDtypeStruct((SPAN, GROUPS, BLOCKS * 16, SUB), jnp.bfloat16),
             jax.ShapeDtypeStruct((SPAN, GROUPS, 3 * BLOCKS * 16, 2 * SUB), jnp.bfloat16),
@@ -270,8 +267,8 @@
     prepare(0)
     for t in range(SPAN):
         sums = (
-            jnp.dot(even_ref[t, 0], rhs[t % 2, :SUB], preferred_element_type=jnp.float32),
-            jnp.dot(rest_ref[t, 0], rhs[t % 2], preferred_element_type=jnp.float32),
+            jnp.dot(even_ref[t, g], rhs[t % 2, :SUB], preferred_element_type=jnp.float32),
+            jnp.dot(rest_ref[t, g], rhs[t % 2], preferred_element_type=jnp.float32),
         )
         if t + 1 < SPAN:
             prepare(t + 1)
@@ -337,18 +334,75 @@
 
     @pl.when(g == GROUPS - 1)
     def _():
-        tiles = out_ref.shape[0]
         others = pl.ds(0, total - 1)
-        for tile in range(tiles):
+        half = lax.axis_size("wa") // 2
+        lane = lax.broadcasted_iota(jnp.int32, (16, LANE), 1)
+        odd32 = (lane // 32) % 2 == 1
+        high64 = lane >= 64
+
+        def regroup(tiles):
+            a, b, c, d = tiles
+            ab0 = jnp.where(odd32, pltpu.roll(b, 32, 1), a)
+            ab1 = jnp.where(odd32, b, pltpu.roll(a, 96, 1))
+            cd0 = jnp.where(odd32, pltpu.roll(d, 32, 1), c)
+            cd1 = jnp.where(odd32, d, pltpu.roll(c, 96, 1))
+            return (
+                jnp.where(high64, pltpu.roll(cd0, 64, 1), ab0),
+                jnp.where(high64, pltpu.roll(cd1, 64, 1), ab1),
+                jnp.where(high64, cd0, pltpu.roll(ab0, 64, 1)),
+                jnp.where(high64, cd1, pltpu.roll(ab1, 64, 1)),
+            )
+
+        def arrived(tile, carry):
             pltpu.make_async_copy(sending.at[tile, me], landing.at[tile, me], local_sem.at[tile]).wait()
             pltpu.make_async_copy(sending.at[tile, others], landing.at[tile, others], recv_sem.at[tile]).wait()
-            pltpu.make_async_copy(landing.at[tile], out_ref.at[tile], local_sem.at[tile]).start()
-        for tile in range(tiles):
+
+            def mirror(w, carry):
+                north, south = (
+                    regroup(
+                        [
+                            landing[tile, (side * half + w) * vert_count + v].astype(jnp.float32)
+                            for v in range(SPAN)
+                        ]
+                    )
+                    for side in range(2)
+                )
+                for kind in range(2):
+                    for t in range(SPAN):
+                        value = north[t] - south[t] if kind else north[t] + south[t]
+                        top = ((w * 2 + kind) * SPAN + t) * dest_rows + tile * 16
+                        spread[pl.ds(pl.multiple_of(top, 16), 16), :] = value
+                return carry
+
+            lax.fori_loop(0, half, mirror, 0)
+            return carry
+
+        lax.fori_loop(0, landing.shape[0], arrived, 0)
+
+        def gather(w, carry):
+            for kind in range(2):
+                for t in range(0, SPAN, 2):
+                    for col in range(per_dest):
+                        both = [
+                            spread[
+                                pl.ds(((w * 2 + kind) * SPAN + t + e) * dest_rows + col, GROUPS, stride=per_dest), :
+                            ]
+                            for e in range(2)
+                        ]
+                        at = ((col % 2) * 2 + kind) * LANE
+                        top = pl.multiple_of(w * SPAN * GROUPS + t * GROUPS, 16)
+                        out_ref[col // 2, pl.ds(top, 16), at : at + LANE] = jnp.concatenate(both, axis=0).astype(
+                            jnp.bfloat16
+                        )
+            return carry
+
+        lax.fori_loop(0, half, gather, 0)
+        for tile in range(landing.shape[0]):
             pltpu.make_async_copy(sending.at[tile, others], landing.at[tile, others], send_sem.at[tile]).wait()
-            pltpu.make_async_copy(landing.at[tile], out_ref.at[tile], local_sem.at[tile]).wait()
 
 
 def fourier_all(row_length, pair_order, even, rest, device_total):
+    lat_pairs = row_length.shape[0] * lax.axis_size("wa") // 2
     tiles = WAVES * GROUPS // device_total // 16
     return pl.pallas_call(
         fourier_kernel,
@@ -356,11 +410,11 @@
         in_specs=[
             pl.BlockSpec(memory_space=pltpu.SMEM),
             pl.BlockSpec((device_total, pair_order.shape[0] // device_total), lambda g: (0, 0)),
-            pl.BlockSpec((SPAN, 1) + even.shape[2:], lambda g: (0, g, 0, 0)),
-            pl.BlockSpec((SPAN, 1) + rest.shape[2:], lambda g: (0, g, 0, 0)),
+            pl.BlockSpec(memory_space=pltpu.VMEM),
+            pl.BlockSpec(memory_space=pltpu.VMEM),
         ],
-        out_specs=pl.BlockSpec(memory_space=pl.ANY),
-        out_shape=jax.ShapeDtypeStruct((tiles, device_total, 16, LANE), jnp.bfloat16),
+        out_specs=pl.BlockSpec(memory_space=pltpu.VMEM),
+        out_shape=jax.ShapeDtypeStruct((WAVES // device_total // 2, lat_pairs, 4 * LANE), jnp.bfloat16),
         scratch_shapes=[
             pltpu.VMEM((2, 2 * SUB, 2 * CPAD), jnp.bfloat16),
             pltpu.VMEM((2, 2, 24, CPAD), jnp.float32),
@@ -380,55 +434,9 @@
     )(row_length, pair_order.reshape(device_total, -1), even, rest)
 
 
-def legendre_kernel(pair_ref, recv_ref, leg_ref, out_ref, operand, loose):
+def legendre_kernel(pair_ref, operand, leg_ref, out_ref):
     slot = pl.program_id(0)
     owner = lax.axis_index("wa") * lax.axis_size("vert") + lax.axis_index("vert")
-
-    @pl.when(slot == 0)
-    def _():
-        lane = lax.broadcasted_iota(jnp.int32, (8, LANE), 1)
-        odd32 = (lane // 32) % 2 == 1
-        high64 = lane >= 64
-        per_dest = loose.shape[2] // GROUPS
-        half = recv_ref.shape[1] // 2
-
-        def regroup(tiles):
-            a, b, c, d = tiles
-            ab0 = jnp.where(odd32, pltpu.roll(b, 32, 1), a)
-            ab1 = jnp.where(odd32, b, pltpu.roll(a, 96, 1))
-            cd0 = jnp.where(odd32, pltpu.roll(d, 32, 1), c)
-            cd1 = jnp.where(odd32, d, pltpu.roll(c, 96, 1))
-            return (
-                jnp.where(high64, pltpu.roll(cd0, 64, 1), ab0),
-                jnp.where(high64, pltpu.roll(cd1, 64, 1), ab1),
-                jnp.where(high64, cd0, pltpu.roll(ab0, 64, 1)),
-                jnp.where(high64, cd1, pltpu.roll(ab1, 64, 1)),
-            )
-
-        def pair(w, carry):
-            for side in range(2):
-                for v in range(4):
-                    for tile in range(recv_ref.shape[0]):
-                        loose[side, v, tile * 16 : tile * 16 + 16, :] = recv_ref[tile, side * half + w, v].astype(
-                            jnp.float32
-                        )
-            for col in range(per_dest):
-                north, south = (
-                    regroup([loose[side, v, pl.ds(col, 8, stride=per_dest), :] for v in range(4)]) for side in range(2)
-                )
-                for t in range(0, 4, 2):
-                    top = pl.multiple_of(w * 32 + t * 8, 16)
-                    sums = [north[t + e] + south[t + e] for e in range(2)]
-                    differences = [north[t + e] - south[t + e] for e in range(2)]
-                    for kind, both in enumerate((sums, differences)):
-                        at = ((col % 2) * 2 + kind) * LANE
-                        operand[col // 2, pl.ds(top, 16), at : at + LANE] = jnp.concatenate(both, axis=0).astype(
-                            jnp.bfloat16
-                        )
-            return carry
-
-        lax.fori_loop(0, half, pair, 0)
-
     first_count = WAVES - pair_ref[owner * pl.num_programs(0) + slot]
     columns = leg_ref.shape[1]
     whole = columns // LANE * LANE
@@ -449,11 +457,11 @@
 
     for start in range(0, whole, PART):
         product = jnp.dot(
-            leg_ref[0, start : start + PART, :], operand[slot], preferred_element_type=jnp.float32
+            leg_ref[slot, start : start + PART, :], operand[slot], preferred_element_type=jnp.float32
         )
         for top in range(0, PART, LANE):
             choose(product[top : top + LANE], start + top, slice(start + top, start + top + LANE))
-    last = leg_ref[0, whole:columns, :]
+    last = leg_ref[slot, whole:columns, :]
     product = jnp.dot(
         jnp.broadcast_to(last, (16, last.shape[1])), operand[slot], preferred_element_type=jnp.float32
     )
@@ -470,29 +478,22 @@
             out_ref[0, i, v * 16 : v * 16 + 16, whole:columns] = turned[at : at + 16, : columns - whole]
 
 
-def legendre_all(received, legendre, pair_order, wa_count, vert_count):
+def legendre_all(operand, legendre, pair_order, vert_count):
     slot_count, lat_pairs, columns = legendre.shape
     field_count = 16 * vert_count
-    tiles = received.shape[0]
-    turned = jnp.swapaxes(legendre, 1, 2)
-    shaped = received.reshape(tiles, wa_count, vert_count, 16, LANE)
     return pl.pallas_call(
         legendre_kernel,
         grid=(slot_count,),
         in_specs=[
             pl.BlockSpec(memory_space=pltpu.SMEM),
-            pl.BlockSpec(shaped.shape, lambda s: (0, 0, 0, 0, 0)),
-            pl.BlockSpec((1, columns, lat_pairs), lambda s: (s, 0, 0)),
+            pl.BlockSpec(memory_space=pltpu.VMEM),
+            pl.BlockSpec(memory_space=pltpu.VMEM),
         ],
         out_specs=pl.BlockSpec((1, 2, field_count, columns), lambda s: (s, 0, 0, 0)),
         out_shape=jax.ShapeDtypeStruct((slot_count, 2, field_count, columns), jnp.float32),
-        scratch_shapes=[
-            pltpu.VMEM((slot_count, lat_pairs, 4 * LANE), jnp.bfloat16),
-            pltpu.VMEM((2, vert_count, tiles * 16, LANE), jnp.float32),
-        ],
         compiler_params=pltpu.CompilerParams(vmem_limit_bytes=24 * 2**20),
         name="legendre",
-    )(pair_order, shaped, turned)
+    )(pair_order, operand, jnp.swapaxes(legendre, 1, 2))
 
 
 def body(grid_values, row_length, pair_order, legendre):
@@ -500,8 +501,8 @@
     vert_count = lax.axis_size("vert")
     device_total = wa_count * vert_count
     even, rest = fold_all(grid_values, row_length)
-    received = fourier_all(row_length, pair_order, even, rest, device_total)
-    return legendre_all(received, legendre, pair_order, wa_count, vert_count)
+    operand = fourier_all(row_length, pair_order, even, rest, device_total)
+    return legendre_all(operand, legendre, pair_order, vert_count)
 
 
 def solution(mesh):

time: 75.7 us -> 73.9 us (0.976)
  Pallas kernels: 71.3 us -> 69.5 us
    pallas_call x1, Pallas kernels: 10.1 us -> 6.57 us  [legendre_all(): pl.pallas_call(legendre_kernel, grid=(slot_count,), in_specs=[pl.BlockSpe...]
    pallas_call x1, Pallas kernels: 51 us -> 54 us  [fourier_all(): pl.pallas_call(fourier_kernel, grid=(GROUPS,), in_specs=[pl.BlockSpec(mem...]
    pallas_call x1, Pallas kernels: 10.2 us -> 8.89 us  [fold_all(): pl.pallas_call(fold_kernel, in_specs=[pl.BlockSpec(memory_space=pltpu.SME...]
where the time goes in v4:
time: 73.9 us; the launch traced here: 73.7 us
  Pallas kernels  69.5 us (94%)
  local copies, waits for them, and re-layouts  4.13 us (6%)
    pallas_call x1, Pallas kernels, fourier_all(): pl.pallas_call(fourier_kernel, grid=(GROUPS,), in_specs=[pl.BlockSpec(mem...  54 us
    pallas_call x1, Pallas kernels, fold_all(): pl.pallas_call(fold_kernel, in_specs=[pl.BlockSpec(memory_space=pltpu.SME...  8.89 us
    pallas_call x1, Pallas kernels, legendre_all(): pl.pallas_call(legendre_kernel, grid=(slot_count,), in_specs=[pl.BlockSpe...  6.57 us
    unnamed x12, local copies, waits for them, and re-layouts  3.24 us

profile of v4, /device:TPU:1, one launch (start us, length us, event | category | flops | bytes accessed | tf_op | source)
XLA Modules:
  0.0 73.7 jit_solution(14330345370589559506)
XLA Ops:
  0.0 0.0 copy-start.3
  0.0 0.9 %reshape.6.order_ref = s32[128,5]{1,0:T(8,128)S(1)} reshape(s32[640]{0:T(1024)} %pair_ref.1) | data formatting | bytes 5120 | tf_op jit(solution)/shard_map/reshape | solution.py:434
  0.9 0.0 copy-start
  0.9 2.6 %copy-done = bf16[32,16,5376]{2,1,0:T(8,128)(2,1)S(1)} copy-done((bf16[32,16,5376]{2,1,0:T(8,128)(2,1)S(1)}, bf16[32,16,5376]{2,1,0:T(8,128)(2,1)}, u32[]{:S(2)}) %copy-start) | copy-done | bytes 5505048
  3.5 0.0 copy-start.2
  3.5 0.7 copy-done.2
  4.1 0.0 slice-start
  4.1 8.9 %fold.1 = (bf16[4,8,96,256]{3,2,1,0:T(8,128)(2,1)S(1)}, bf16[4,8,288,512]{3,2,1,0:T(8,128)(2,1)S(1)}) custom-call(s32[32]{0:T(128)S(1)} %copy-done.2, bf16[4,8,16,5376]{3,2,1,0:T(8,128)(2,1)S(1)} %bitcast.5), custom_call_target="tpu_custom_call" | custom-call | tf_op jit(solution)/shard_map/fold/pallas_call | solution.py:149
  13.0 0.0 copy-done.3
  13.0 0.0 slice-start.1
  13.0 0.0 copy-start.1
  13.1 54.0 %fourier.1.operand = bf16[5,512,512]{2,1,0:T(8,128)(2,1)S(1)} custom-call(s32[32]{0:T(128)S(1)} %copy-done.3, s32[128,5]{1,0:T(8,128)S(1)} %reshape.6.order_ref, bf16[4,8,96,256]{3,2,1,0:T(8,128)(2,1)S(1)} %get-tuple-element.7.even_ref, bf16[4,8,288,512]{3,2,1,0:T(8,128)(2,1)S(1)} %get-tuple-element.8.rest_ref), custom_call_target="tpu_custom_call" | custom-call | tf_op jit(solution)/shard_map/fourier/pallas_call | solution.py:407
  67.1 0.0 slice-done
  67.1 0.0 slice-done.1
  67.1 0.0 copy-done.1
  67.1 6.6 %legendre.1 = f32[5,2,64,1281]{3,2,1,0:T(8,128)} custom-call(s32[640]{0:T(1024)S(1)} %copy-done.1, bf16[5,512,512]{2,1,0:T(8,128)(2,1)S(1)} %fourier.1.operand, bf16[5,1281,512]{2,1,0:T(8,128)(2,1)S(1)} %bitcast.4), custom_call_target="tpu_custom_call" | custom-call | tf_op jit(solution)/shard_map/legendre/pallas_call | solution.py:484
  (1 shorter events, 0.0 us)
Async XLA Ops:
  0.0 13.0 %copy-start.3 = (s32[32]{0:T(128)S(1)}, s32[32]{0:T(128)}, u32[]{:S(2)}) copy-start(s32[32]{0:T(128)} %length_ref.3) | copy-start | bytes 388
  0.9 2.6 %copy-start = (bf16[32,16,5376]{2,1,0:T(8,128)(2,1)S(1)}, bf16[32,16,5376]{2,1,0:T(8,128)(2,1)}, u32[]{:S(2)}) copy-start(bf16[32,16,5376]{2,1,0:T(8,128)(2,1)} %param.4) | copy-start | bytes 16515076
  3.5 0.7 copy-start.2
  4.1 62.9 %slice-start = ((s8[6594560]{0:T(1024)(128)(4,1)}), s8[4194304]{0:T(1024)(128)(4,1)S(1)}, s32[]{:S(2)}) async-start(s8[6594560]{0:T(1024)(128)(4,1)} %bitcast.2), calls=%async_computation | async-start | bytes 8388608
  13.0 54.0 %slice-start.1 = ((s8[6594560]{0:T(1024)(128)(4,1)}), s8[2400256]{0:T(1024)(128)(4,1)S(1)}, s32[]{:S(2)}) async-start(s8[6594560]{0:T(1024)(128)(4,1)} %bitcast.2), calls=%async_computation.1 | async-start | bytes 4800512
  13.0 54.0 %copy-start.1 = (s32[640]{0:T(1024)S(1)}, s32[640]{0:T(1024)}, u32[]{:S(2)}) copy-start(s32[640]{0:T(1024)} %pair_ref.1) | copy-start | bytes 7684

commit v5 on v4

--- a/solution.py
+++ b/solution.py
@@ -51,121 +51,15 @@
     return lax.broadcasted_iota(jnp.int32, shape, dim).astype(jnp.float32)
 
 
-def fold_kernel(length_ref, grid_ref, even_ref, rest_ref, twiddle):
-    def eight_rows(block, carry):
-        sub = lax.broadcasted_iota(jnp.int32, (8, LANE), 0)
-        n8 = jnp.zeros((8, LANE), jnp.int32)
-        for e in range(8):
-            n8 = jnp.where(sub == e, length_ref[block * 8 + e] // 4, n8)
-        inv8 = 0.25 / n8.astype(jnp.float32)
-        for j in range(CHUNKS):
-            k = lax.broadcasted_iota(jnp.int32, (8, LANE), 1) + j * LANE
-            c1, s1 = sincos(k.astype(jnp.float32) * inv8)
-            c2 = c1 * c1 - s1 * s1
-            s2 = 2.0 * c1 * s1
-            c3 = c2 * c1 - s2 * s1
-            s3 = s2 * c1 + c2 * s1
-            inside = k < n8
-            for which, v in enumerate((c1, s1, c2, s2, c3, s3)):
-                v = jnp.where(inside, v, 0.0)
-                for e in range(8):
-                    twiddle[block * 8 + e, which : which + 1, j * LANE : (j + 1) * LANE] = v[e : e + 1]
-        return carry
-
-    lax.fori_loop(0, twiddle.shape[0] // 8, eight_rows, 0)
-
-    lane = lax.broadcasted_iota(jnp.int32, (16, LANE), 1)
-    zero = jnp.zeros((16, LANE), jnp.bfloat16)
-
-    def one_row(t, g):
-        row = t * GROUPS + g
-        n = length_ref[row] // 4
-        starts = []
-        for part in range(4):
-            start = n * part
-            whole = start // LANE
-            shift = start - whole * LANE
-            starts.append((whole, shift, lax.rem(LANE - shift, LANE)))
-
-        def piece(part, j):
-            whole, shift, back = starts[part]
-            at = pl.multiple_of((whole + j) * LANE, LANE)
-            value = grid_ref[t, g, :, pl.ds(at, LANE)].astype(jnp.float32)
-            return pltpu.roll(value, back, 1) if part else value
-
-        held = [piece(part, 0) for part in range(4)]
-        for j in range(CHUNKS):
-            inside = lane + j * LANE < n
-            quarter = []
-            for part in range(4):
-                value = held[part]
-                following = piece(part, j + 1) if part or j + 1 < CHUNKS else None
-                if part:
-                    value = jnp.where(lane < LANE - starts[part][1], value, following)
-                held[part] = following
-                quarter.append(value)
-            c1, s1, c2, s2, c3, s3 = (
-                twiddle[row, which : which + 1, j * LANE : (j + 1) * LANE] for which in range(6)
-            )
-            qa, qb, qc, qd = quarter
-            even = qa + qc
-            even_other = qb + qd
-            re = qa - qc
-            im = qd - qb
-            h2 = even - even_other
-            q = j // 2
-            at = (j % 2) * LANE
-            even_ref[t, g, q * 16 : q * 16 + 16, at : at + LANE] = jnp.where(
-                inside, even + even_other, 0.0
-            ).astype(jnp.bfloat16)
-            values = (
-                (re * c1 + im * s1, im * c1 - re * s1),
-                (h2 * c2, -(h2 * s2)),
-                (re * c3 - im * s3, -(im * c3 + re * s3)),
-            )
-            for r, (zr, zi) in enumerate(values):
-                top = (r * BLOCKS + q) * 16
-                rest_ref[t, g, top : top + 16, at : at + LANE] = zr.astype(jnp.bfloat16)
-                rest_ref[t, g, top : top + 16, SUB + at : SUB + at + LANE] = zi.astype(jnp.bfloat16)
-        for j in range(CHUNKS, 2 * BLOCKS):
-            q = j // 2
-            at = (j % 2) * LANE
-            even_ref[t, g, q * 16 : q * 16 + 16, at : at + LANE] = zero
-            for r in range(3):
-                top = (r * BLOCKS + q) * 16
-                rest_ref[t, g, top : top + 16, at : at + LANE] = zero
-                rest_ref[t, g, top : top + 16, SUB + at : SUB + at + LANE] = zero
-        return g
-
-    def one_group(g, carry):
-        lax.fori_loop(0, SPAN, one_row, g)
-        return carry
-
-    lax.fori_loop(0, GROUPS, one_group, 0)
-
-
-def fold_all(grid_values, row_length):
-    row_total, field_count, points = grid_values.shape
-    return pl.pallas_call(
-        fold_kernel,
-        in_specs=[pl.BlockSpec(memory_space=pltpu.SMEM), pl.BlockSpec(memory_space=pltpu.VMEM)],
-        out_specs=[pl.BlockSpec(memory_space=pltpu.VMEM)] * 2,
-        out_shape=[
-            jax.ShapeDtypeStruct((SPAN, GROUPS, BLOCKS * 16, SUB), jnp.bfloat16),
-            jax.ShapeDtypeStruct((SPAN, GROUPS, 3 * BLOCKS * 16, 2 * SUB), jnp.bfloat16),
-        ],
-        scratch_shapes=[pltpu.VMEM((row_total, 8, CHUNKS * LANE), jnp.float32)],
-        compiler_params=pltpu.CompilerParams(vmem_limit_bytes=16 * 2**20),
-        name="fold",
-    )(row_length, grid_values.reshape(SPAN, GROUPS, field_count, points))
-
-
 def fourier_kernel(
     length_ref,
     order_ref,
-    even_ref,
-    rest_ref,
+    grid_ref,
     out_ref,
+    chunked,
+    twiddle,
+    even,
+    rest,
     rhs,
     small,
     onehot,
@@ -187,8 +81,33 @@
     def place(device):
         return (device // vert_count, lax.rem(device, vert_count))
 
+    @pl.when(g % 2 == 0)
+    def _():
+        sub = lax.broadcasted_iota(jnp.int32, (8, LANE), 0)
+        n8 = jnp.zeros((8, LANE), jnp.int32)
+        for e in range(8):
+            n8 = jnp.where(sub == e, length_ref[(e // 2) * GROUPS + g + e % 2] // 4, n8)
+        inv8 = 0.25 / n8.astype(jnp.float32)
+        for j in range(CHUNKS):
+            k = lax.broadcasted_iota(jnp.int32, (8, LANE), 1) + j * LANE
+            c1, s1 = sincos(k.astype(jnp.float32) * inv8)
+            c2 = c1 * c1 - s1 * s1
+            s2 = 2.0 * c1 * s1
+            c3 = c2 * c1 - s2 * s1
+            s3 = s2 * c1 + c2 * s1
+            inside = k < n8
+            for which, v in enumerate((c1, s1, c2, s2, c3, s3)):
+                v = jnp.where(inside, v, 0.0)
+                for e in range(8):
+                    twiddle[e, which : which + 1, j * LANE : (j + 1) * LANE] = v[e : e + 1]
+
     @pl.when(g == 0)
     def _():
+        for slot in range(2):
+            for q in range(BLOCKS):
+                even[slot, q * 16 : q * 16 + 16, :] = jnp.zeros((16, SUB), jnp.bfloat16)
+            for top in range(0, 3 * BLOCKS * 16, 16):
+                rest[slot, top : top + 16, :] = jnp.zeros((16, 2 * SUB), jnp.bfloat16)
         barrier = pltpu.get_barrier_semaphore()
 
         def greet(i, carry):
@@ -207,7 +126,51 @@
                     (wave == target).astype(jnp.float32).astype(jnp.bfloat16)
                 )
 
+    def fold(t):
+        slot = t % 2
+        n = length_ref[t * GROUPS + g] // 4
+        for j in range(grid_ref.shape[3] // LANE):
+            chunked[slot, j] = grid_ref[t, 0, :, j * LANE : (j + 1) * LANE]
+        difference = lax.broadcasted_iota(jnp.int32, (2 * LANE, LANE), 0) - lax.broadcasted_iota(
+            jnp.int32, (2 * LANE, LANE), 1
+        )
+        quarters = [[chunked[slot, j].astype(jnp.float32) for j in range(CHUNKS)]]
+        for part in range(1, 4):
+            start = n * part
+            whole = start // LANE
+            pick = (difference == start - whole * LANE).astype(jnp.float32).astype(jnp.bfloat16)
+            pieces = [chunked[slot, whole + j] for j in range(CHUNKS + 1)]
+            pairs = [jnp.concatenate([pieces[j], pieces[j + 1]], axis=1) for j in range(CHUNKS)]
+            moved = jnp.dot(jnp.concatenate(pairs, axis=0), pick, preferred_element_type=jnp.float32)
+            quarters.append([moved[j * 16 : j * 16 + 16] for j in range(CHUNKS)])
+        lane = lax.broadcasted_iota(jnp.int32, (16, LANE), 1)
+        for j in range(CHUNKS):
+            c1, s1, c2, s2, c3, s3 = (
+                twiddle[t * 2 + g % 2, which : which + 1, j * LANE : (j + 1) * LANE] for which in range(6)
+            )
+            qa, qb, qc, qd = (quarters[part][j] for part in range(4))
+            even_sum = qa + qc
+            odd_sum = qb + qd
+            re = qa - qc
+            im = qd - qb
+            h2 = even_sum - odd_sum
+            q = j // 2
+            at = (j % 2) * LANE
+            even[slot, q * 16 : q * 16 + 16, at : at + LANE] = jnp.where(
+                lane + j * LANE < n, even_sum + odd_sum, 0.0
+            ).astype(jnp.bfloat16)
+            values = (
+                (re * c1 + im * s1, im * c1 - re * s1),
+                (h2 * c2, -(h2 * s2)),
+                (re * c3 - im * s3, -(im * c3 + re * s3)),
+            )
+            for r, (zr, zi) in enumerate(values):
+                top = (r * BLOCKS + q) * 16
+                rest[slot, top : top + 16, at : at + LANE] = zr.astype(jnp.bfloat16)
+                rest[slot, top : top + 16, SUB + at : SUB + at + LANE] = zi.astype(jnp.bfloat16)
+
     def prepare(t):
+        fold(t)
         slot = t % 2
         n = jnp.full((8, CPAD), length_ref[t * GROUPS + g] // 4, jnp.int32)
         n_float = n.astype(jnp.float32)
@@ -267,8 +230,8 @@
     prepare(0)
     for t in range(SPAN):
         sums = (
-            jnp.dot(even_ref[t, g], rhs[t % 2, :SUB], preferred_element_type=jnp.float32),
-            jnp.dot(rest_ref[t, g], rhs[t % 2], preferred_element_type=jnp.float32),
+            jnp.dot(even[t % 2], rhs[t % 2, :SUB], preferred_element_type=jnp.float32),
+            jnp.dot(rest[t % 2], rhs[t % 2], preferred_element_type=jnp.float32),
         )
         if t + 1 < SPAN:
             prepare(t + 1)
@@ -374,7 +337,7 @@
                         spread[pl.ds(pl.multiple_of(top, 16), 16), :] = value
                 return carry
 
-            lax.fori_loop(0, half, mirror, 0)
+            lax.fori_loop(0, half, mirror, 0, unroll=4)
             return carry
 
         lax.fori_loop(0, landing.shape[0], arrived, 0)
@@ -401,7 +364,8 @@
             pltpu.make_async_copy(sending.at[tile, others], landing.at[tile, others], send_sem.at[tile]).wait()
 
 
-def fourier_all(row_length, pair_order, even, rest, device_total):
+def fourier_all(row_length, pair_order, grid_values, device_total):
+    row_total, field_count, points = grid_values.shape
     lat_pairs = row_length.shape[0] * lax.axis_size("wa") // 2
     tiles = WAVES * GROUPS // device_total // 16
     return pl.pallas_call(
@@ -410,12 +374,15 @@
         in_specs=[
             pl.BlockSpec(memory_space=pltpu.SMEM),
             pl.BlockSpec((device_total, pair_order.shape[0] // device_total), lambda g: (0, 0)),
-            pl.BlockSpec(memory_space=pltpu.VMEM),
-            pl.BlockSpec(memory_space=pltpu.VMEM),
+            pl.BlockSpec((SPAN, 1, field_count, points), lambda g: (0, g, 0, 0)),
         ],
         out_specs=pl.BlockSpec(memory_space=pltpu.VMEM),
         out_shape=jax.ShapeDtypeStruct((WAVES // device_total // 2, lat_pairs, 4 * LANE), jnp.bfloat16),
         scratch_shapes=[
+            pltpu.VMEM((2, points // LANE, 16, LANE), jnp.bfloat16),
+            pltpu.VMEM((8, 8, CHUNKS * LANE), jnp.float32),
+            pltpu.VMEM((2, BLOCKS * 16, SUB), jnp.bfloat16),
+            pltpu.VMEM((2, 3 * BLOCKS * 16, 2 * SUB), jnp.bfloat16),
             pltpu.VMEM((2, 2 * SUB, 2 * CPAD), jnp.bfloat16),
             pltpu.VMEM((2, 2, 24, CPAD), jnp.float32),
             pltpu.VMEM((WAVES, 4 * CPAD), jnp.bfloat16),
@@ -428,10 +395,10 @@
             pltpu.SemaphoreType.DMA((tiles,)),
         ],
         compiler_params=pltpu.CompilerParams(
-            vmem_limit_bytes=34 * 2**20, collective_id=0, has_side_effects=True
+            vmem_limit_bytes=48 * 2**20, collective_id=0, has_side_effects=True
         ),
         name="fourier",
-    )(row_length, pair_order.reshape(device_total, -1), even, rest)
+    )(row_length, pair_order.reshape(device_total, -1), grid_values.reshape(SPAN, GROUPS, field_count, points))
 
 
 def legendre_kernel(pair_ref, operand, leg_ref, out_ref):
@@ -500,8 +467,7 @@
     wa_count = lax.axis_size("wa")
     vert_count = lax.axis_size("vert")
     device_total = wa_count * vert_count
-    even, rest = fold_all(grid_values, row_length)
-    operand = fourier_all(row_length, pair_order, even, rest, device_total)
+    operand = fourier_all(row_length, pair_order, grid_values, device_total)
     return legendre_all(operand, legendre, pair_order, vert_count)
 
 

time: 73.9 us -> 68.1 us (0.922)
  Pallas kernels: 69.5 us -> 66.3 us
  local copies, waits for them, and re-layouts: 4.13 us -> 1.61 us
    pallas_call x1 -> x0, Pallas kernels: 8.89 us -> none  [fold_all(): pl.pallas_call(fold_kernel, in_specs=[pl.BlockSpec(memory_space=pltpu.SME...]
    pallas_call x1, Pallas kernels: 54 us -> 59.7 us  [fourier_all(): pl.pallas_call(fourier_kernel, grid=(GROUPS,), in_specs=[pl.BlockSpec(mem...]
    unnamed x12 -> x6, local copies, waits for them, and re-layouts: 3.24 us -> 0.66 us
where the time goes in v5:
time: 68.1 us; the launch traced here: 67.9 us
  Pallas kernels  66.3 us (97%)
  local copies, waits for them, and re-layouts  1.61 us (2%)
    pallas_call x1, Pallas kernels, fourier_all(): pl.pallas_call(fourier_kernel, grid=(GROUPS,), in_specs=[pl.BlockSpec(mem...  59.7 us
    pallas_call x1, Pallas kernels, legendre_all(): pl.pallas_call(legendre_kernel, grid=(slot_count,), in_specs=[pl.BlockSpe...  6.57 us

profile of v5, /device:TPU:1, one launch (start us, length us, event | category | flops | bytes accessed | tf_op | source)
XLA Modules:
  0.0 67.9 jit_solution(14758697994113375619)
XLA Ops:
  0.0 0.0 copy-start.1
  0.0 0.9 %reshape.6.order_ref = s32[128,5]{1,0:T(8,128)S(1)} reshape(s32[640]{0:T(1024)} %pair_ref.1) | data formatting | bytes 5120 | tf_op jit(solution)/shard_map/reshape | solution.py:401
  1.0 0.0 copy-start.2
  1.0 0.6 copy-done.2
  1.6 0.0 copy-start
  1.6 59.7 %fourier.1.operand = bf16[5,512,512]{2,1,0:T(8,128)(2,1)S(1)} custom-call(s32[32]{0:T(128)S(1)} %copy-done.2, s32[128,5]{1,0:T(8,128)S(1)} %reshape.6.order_ref, bf16[4,8,16,5376]{3,2,1,0:T(8,128)(2,1)} %bitcast.3), custom_call_target="tpu_custom_call" | custom-call | tf_op jit(solution)/shard_map/fourier/pallas_call | solution.py:371
  61.3 0.0 copy-done.1
  61.4 0.0 copy-done
  61.4 6.6 %legendre.1 = f32[5,2,64,1281]{3,2,1,0:T(8,128)} custom-call(s32[640]{0:T(1024)S(1)} %copy-done.1, bf16[5,512,512]{2,1,0:T(8,128)(2,1)S(1)} %fourier.1.operand, bf16[5,1281,512]{2,1,0:T(8,128)(2,1)S(1)} %bitcast.2), custom_call_target="tpu_custom_call" | custom-call | tf_op jit(solution)/shard_map/legendre/pallas_call | solution.py:451
Async XLA Ops:
  0.0 61.3 %copy-start.1 = (s32[640]{0:T(1024)S(1)}, s32[640]{0:T(1024)}, u32[]{:S(2)}) copy-start(s32[640]{0:T(1024)} %pair_ref.1) | copy-start | bytes 7684
  1.0 0.7 copy-start.2
  1.6 59.7 %copy-start = (bf16[5,512,1281]{1,2,0:T(8,128)(2,1)S(1)}, bf16[5,512,1281]{1,2,0:T(8,128)(2,1)}, u32[]{:S(2)}) copy-start(bf16[5,512,1281]{1,2,0:T(8,128)(2,1)} %param.7) | copy-start | bytes 19676164

commit v6 on v5

--- a/solution.py
+++ b/solution.py
@@ -116,35 +116,33 @@
             return carry
 
         lax.fori_loop(1, total, greet, 0)
+        at = lax.broadcasted_iota(jnp.int32, (total, WAVES), 1)
+        kind = (at >= CLASS).astype(jnp.int32) + (at >= 2 * CLASS).astype(jnp.int32) + (at >= 3 * CLASS).astype(jnp.int32)
+        wave = 4 * (at - CLASS * kind) + kind
         for c in range(per_dest):
             pair = order_ref[:, c // 2 : c // 2 + 1]
             target = TRUNC - pair if c % 2 else pair
-            for r in range(4):
-                wave = lax.broadcasted_iota(jnp.int32, (total, CPAD), 1) * 4 + r
-                wave = jnp.where(wave < WAVES, wave, -1)
-                onehot[c * total : (c + 1) * total, r * CPAD : (r + 1) * CPAD] = (
-                    (wave == target).astype(jnp.float32).astype(jnp.bfloat16)
-                )
+            onehot[c * total : (c + 1) * total, :] = (wave == target).astype(jnp.float32).astype(jnp.bfloat16)
+
+    def blocks_of(t):
+        return BLOCKS if t == SPAN - 1 else BLOCKS - 1
 
     def fold(t):
         slot = t % 2
+        chunks = min(CHUNKS, 2 * blocks_of(t))
         n = length_ref[t * GROUPS + g] // 4
         for j in range(grid_ref.shape[3] // LANE):
             chunked[slot, j] = grid_ref[t, 0, :, j * LANE : (j + 1) * LANE]
-        difference = lax.broadcasted_iota(jnp.int32, (2 * LANE, LANE), 0) - lax.broadcasted_iota(
-            jnp.int32, (2 * LANE, LANE), 1
-        )
-        quarters = [[chunked[slot, j].astype(jnp.float32) for j in range(CHUNKS)]]
+        lane = lax.broadcasted_iota(jnp.int32, (16, LANE), 1)
+        quarters = [[chunked[slot, j].astype(jnp.float32) for j in range(chunks)]]
         for part in range(1, 4):
             start = n * part
             whole = start // LANE
-            pick = (difference == start - whole * LANE).astype(jnp.float32).astype(jnp.bfloat16)
-            pieces = [chunked[slot, whole + j] for j in range(CHUNKS + 1)]
-            pairs = [jnp.concatenate([pieces[j], pieces[j + 1]], axis=1) for j in range(CHUNKS)]
-            moved = jnp.dot(jnp.concatenate(pairs, axis=0), pick, preferred_element_type=jnp.float32)
-            quarters.append([moved[j * 16 : j * 16 + 16] for j in range(CHUNKS)])
-        lane = lax.broadcasted_iota(jnp.int32, (16, LANE), 1)
-        for j in range(CHUNKS):
+            back = LANE - (start - whole * LANE)
+            pieces = [chunked[slot, whole + j].astype(jnp.float32) for j in range(chunks + 1)]
+            turned = [pltpu.roll(piece, lax.rem(back, LANE), 1) for piece in pieces]
+            quarters.append([jnp.where(lane < back, turned[j], turned[j + 1]) for j in range(chunks)])
+        for j in range(chunks):
             c1, s1, c2, s2, c3, s3 = (
                 twiddle[t * 2 + g % 2, which : which + 1, j * LANE : (j + 1) * LANE] for which in range(6)
             )
@@ -165,7 +163,7 @@
                 (re * c3 - im * s3, -(im * c3 + re * s3)),
             )
             for r, (zr, zi) in enumerate(values):
-                top = (r * BLOCKS + q) * 16
+                top = (q * 3 + r) * 16
                 rest[slot, top : top + 16, at : at + LANE] = zr.astype(jnp.bfloat16)
                 rest[slot, top : top + 16, SUB + at : SUB + at + LANE] = zi.astype(jnp.bfloat16)
 
@@ -210,12 +208,13 @@
         scale = 1.0 / jnp.sqrt(length.astype(jnp.float32))
         column = lax.broadcasted_iota(jnp.int32, (1, CPAD), 1)
         lane_top = pl.multiple_of(jnp.where(paired, LANE, 0) + t * 32, 32)
+        left = [None, None]
         for r in range(4):
-            part_sum, first = (sums[0], 0) if r == 0 else (sums[1], (r - 1) * 96)
+            part_sum, first, step = (sums[0], 0, 16) if r == 0 else (sums[1], (r - 1) * 16, 48)
             real = part_sum[first : first + 16, :CPAD]
             imag = part_sum[first : first + 16, CPAD:]
-            for q in range(1, BLOCKS):
-                top = first + q * 16
+            for q in range(1, blocks_of(t)):
+                top = first + q * step
                 pr = part_sum[top : top + 16, :CPAD]
                 pi = part_sum[top : top + 16, CPAD:]
                 c = small[slot, 0, 17 + q : 18 + q, :]
@@ -224,14 +223,21 @@
                 imag = imag + (pi * c - pr * s)
             wave = column * 4 + r
             keep = jnp.where((wave * 2 <= length - 1) & (column < CLASS), scale, 0.0)
-            rows[pl.ds(lane_top, 16), r * CPAD : (r + 1) * CPAD] = (real * keep).astype(jnp.bfloat16)
-            rows[pl.ds(lane_top + 16, 16), r * CPAD : (r + 1) * CPAD] = (imag * keep).astype(jnp.bfloat16)
+            for i, value in enumerate((real * keep, imag * keep)):
+                if r % 2 == 0:
+                    left[i] = value
+                    continue
+                right = pltpu.roll(value, CPAD - CLASS, 1)
+                middle = left[i][:, 2 * LANE :] + right[:, :LANE]
+                packed = jnp.concatenate([left[i][:, : 2 * LANE], middle, right[:, LANE:]], axis=1)
+                at = (r // 2) * 2 * CLASS
+                rows[pl.ds(lane_top + i * 16, 16), at : at + 2 * CLASS] = packed.astype(jnp.bfloat16)
 
     prepare(0)
     for t in range(SPAN):
         sums = (
-            jnp.dot(even[t % 2], rhs[t % 2, :SUB], preferred_element_type=jnp.float32),
-            jnp.dot(rest[t % 2], rhs[t % 2], preferred_element_type=jnp.float32),
+            jnp.dot(even[t % 2, : blocks_of(t) * 16], rhs[t % 2, :SUB], preferred_element_type=jnp.float32),
+            jnp.dot(rest[t % 2, : blocks_of(t) * 48], rhs[t % 2], preferred_element_type=jnp.float32),
         )
         if t + 1 < SPAN:
             prepare(t + 1)
@@ -385,8 +391,8 @@
             pltpu.VMEM((2, 3 * BLOCKS * 16, 2 * SUB), jnp.bfloat16),
             pltpu.VMEM((2, 2 * SUB, 2 * CPAD), jnp.bfloat16),
             pltpu.VMEM((2, 2, 24, CPAD), jnp.float32),
-            pltpu.VMEM((WAVES, 4 * CPAD), jnp.bfloat16),
-            pltpu.VMEM((2 * LANE, 4 * CPAD), jnp.bfloat16),
+            pltpu.VMEM((WAVES, WAVES), jnp.bfloat16),
+            pltpu.VMEM((2 * LANE, WAVES), jnp.bfloat16),
             pltpu.VMEM((WAVES * GROUPS, LANE), jnp.float32),
             pltpu.VMEM((tiles, device_total, 16, LANE), jnp.bfloat16),
             pltpu.VMEM((tiles, device_total, 16, LANE), jnp.bfloat16),

time: 68.1 us -> 64.9 us (0.953)
  Pallas kernels: 66.3 us -> 63.1 us
    pallas_call x1, Pallas kernels: 59.7 us -> 56.6 us  [fourier_all(): pl.pallas_call(fourier_kernel, grid=(GROUPS,), in_specs=[pl.BlockSpec(mem...]
where the time goes in v6:
time: 64.9 us; the launch traced here: 64.8 us
  Pallas kernels  63.1 us (97%)
  local copies, waits for them, and re-layouts  1.61 us (2%)
    pallas_call x1, Pallas kernels, fourier_all(): pl.pallas_call(fourier_kernel, grid=(GROUPS,), in_specs=[pl.BlockSpec(mem...  56.6 us
    pallas_call x1, Pallas kernels, legendre_all(): pl.pallas_call(legendre_kernel, grid=(slot_count,), in_specs=[pl.BlockSpe...  6.57 us

profile of v6, /device:TPU:1, one launch (start us, length us, event | category | flops | bytes accessed | tf_op | source)
XLA Modules:
  0.0 64.8 jit_solution(8557219916222105682)
XLA Ops:
  0.0 0.0 copy-start.1
  0.0 0.9 %reshape.6.order_ref = s32[128,5]{1,0:T(8,128)S(1)} reshape(s32[640]{0:T(1024)} %pair_ref.1) | data formatting | bytes 5120 | tf_op jit(solution)/shard_map/reshape | solution.py:407
  1.0 0.0 copy-start.2
  1.0 0.6 %copy-done.2 = s32[32]{0:T(128)S(1)} copy-done((s32[32]{0:T(128)S(1)}, s32[32]{0:T(128)}, u32[]{:S(2)}) %copy-start.2) | copy-done | bytes 152
  1.6 0.0 copy-start
  1.6 56.6 %fourier.1.operand = bf16[5,512,512]{2,1,0:T(8,128)(2,1)S(1)} custom-call(s32[32]{0:T(128)S(1)} %copy-done.2, s32[128,5]{1,0:T(8,128)S(1)} %reshape.6.order_ref, bf16[4,8,16,5376]{3,2,1,0:T(8,128)(2,1)} %bitcast.3), custom_call_target="tpu_custom_call" | custom-call | tf_op jit(solution)/shard_map/fourier/pallas_call | solution.py:377
  58.2 0.0 copy-done.1
  58.2 0.0 copy-done
  58.2 6.6 %legendre.1 = f32[5,2,64,1281]{3,2,1,0:T(8,128)} custom-call(s32[640]{0:T(1024)S(1)} %copy-done.1, bf16[5,512,512]{2,1,0:T(8,128)(2,1)S(1)} %fourier.1.operand, bf16[5,1281,512]{2,1,0:T(8,128)(2,1)S(1)} %bitcast.2), custom_call_target="tpu_custom_call" | custom-call | tf_op jit(solution)/shard_map/legendre/pallas_call | solution.py:457
Async XLA Ops:
  0.0 58.2 %copy-start.1 = (s32[640]{0:T(1024)S(1)}, s32[640]{0:T(1024)}, u32[]{:S(2)}) copy-start(s32[640]{0:T(1024)} %pair_ref.1) | copy-start | bytes 7684
  1.0 0.7 %copy-start.2 = (s32[32]{0:T(128)S(1)}, s32[32]{0:T(128)}, u32[]{:S(2)}) copy-start(s32[32]{0:T(128)} %length_ref.1) | copy-start | bytes 388
  1.6 56.6 %copy-start = (bf16[5,512,1281]{1,2,0:T(8,128)(2,1)S(1)}, bf16[5,512,1281]{1,2,0:T(8,128)(2,1)}, u32[]{:S(2)}) copy-start(bf16[5,512,1281]{1,2,0:T(8,128)(2,1)} %param.7) | copy-start | bytes 19676164

commit v7 on v6

--- a/solution.py
+++ b/solution.py
@@ -21,7 +21,7 @@
 SPAN = 4
 ORDER = 5
 STRIDE = 13
-PART = 640
+PART = 256
 
 
 def sincos(turns):
@@ -78,9 +78,6 @@
     dest_rows = WAVES * GROUPS // total
     per_dest = WAVES // total
 
-    def place(device):
-        return (device // vert_count, lax.rem(device, vert_count))
-
     @pl.when(g % 2 == 0)
     def _():
         sub = lax.broadcasted_iota(jnp.int32, (8, LANE), 0)
@@ -103,19 +100,28 @@
 
     @pl.when(g == 0)
     def _():
-        for slot in range(2):
-            for q in range(BLOCKS):
-                even[slot, q * 16 : q * 16 + 16, :] = jnp.zeros((16, SUB), jnp.bfloat16)
-            for top in range(0, 3 * BLOCKS * 16, 16):
-                rest[slot, top : top + 16, :] = jnp.zeros((16, 2 * SUB), jnp.bfloat16)
-        barrier = pltpu.get_barrier_semaphore()
+        last = BLOCKS - 1
+        even[1, last * 16 :, LANE:] = jnp.zeros((16, LANE), jnp.bfloat16)
+        for side in range(2):
+            rest[1, last * 48 :, side * SUB + LANE : (side + 1) * SUB] = jnp.zeros((48, LANE), jnp.bfloat16)
+        wa_count = lax.axis_size("wa")
+        wa, vert = lax.axis_index("wa"), lax.axis_index("vert")
+
+        def signal(to_wa, to_vert):
+            pl.semaphore_signal(
+                pltpu.get_barrier_semaphore(), 1, device_id=(to_wa, to_vert), device_id_type=pl.DeviceIdType.MESH
+            )
+
+        for i in range(1, vert_count):
+            signal(wa, lax.rem(vert + i, vert_count))
 
         def greet(i, carry):
-            other = lax.rem(me + i, total)
-            pl.semaphore_signal(barrier, 1, device_id=place(other), device_id_type=pl.DeviceIdType.MESH)
+            to_wa = lax.rem(wa + i, wa_count)
+            for to_vert in range(vert_count):
+                signal(to_wa, to_vert)
             return carry
 
-        lax.fori_loop(1, total, greet, 0)
+        lax.fori_loop(1, wa_count, greet, 0)
         at = lax.broadcasted_iota(jnp.int32, (total, WAVES), 1)
         kind = (at >= CLASS).astype(jnp.int32) + (at >= 2 * CLASS).astype(jnp.int32) + (at >= 3 * CLASS).astype(jnp.int32)
         wave = 4 * (at - CLASS * kind) + kind
@@ -414,26 +420,35 @@
     columns = leg_ref.shape[1]
     whole = columns // LANE * LANE
 
-    def choose(product, top, out_lanes):
-        height = product.shape[0]
-        column = lax.broadcasted_iota(jnp.int32, (height, LANE), 0) + top
-        in_first = column < first_count
-        degree = jnp.where(in_first, column, column - first_count)
-        even = degree % 2 == 0
-        s0, a0, s1, a1 = (product[:, k * LANE : (k + 1) * LANE] for k in range(4))
-        chosen = jnp.where(in_first, jnp.where(even, s0, a0), jnp.where(even, s1, a1))
-        turned = chosen.T
-        for v in range(4):
-            for i in range(2):
-                at = v * 32 + i * 16
-                out_ref[0, i, v * 16 : v * 16 + 16, out_lanes] = turned[at : at + 16]
-
-    for start in range(0, whole, PART):
+    def block(top, group, base):
         product = jnp.dot(
-            leg_ref[slot, start : start + PART, :], operand[slot], preferred_element_type=jnp.float32
+            leg_ref[slot, pl.ds(top, PART), :],
+            operand[slot, :, pl.ds(pl.multiple_of(group * 2 * LANE, 2 * LANE), 2 * LANE)],
+            preferred_element_type=jnp.float32,
         )
-        for top in range(0, PART, LANE):
-            choose(product[top : top + LANE], start + top, slice(start + top, start + top + LANE))
+        column = lax.broadcasted_iota(jnp.int32, (PART, LANE), 0) + (top - base)
+        return jnp.where(column % 2 == 0, product[:, :LANE], product[:, LANE:]).T
+
+    def each_field():
+        return [(i, v * 16, v * 32 + i * 16) for v in range(4) for i in range(2)]
+
+    for top in range(0, whole, PART):
+        second = (top >= first_count).astype(jnp.int32)
+        turned = block(top, second, second * first_count)
+        for i, field, at in each_field():
+            out_ref[0, i, field : field + 16, top : top + PART] = turned[at : at + 16]
+
+    @pl.when(first_count % PART != 0)
+    def _():
+        top = pl.multiple_of(first_count // PART * PART, PART)
+        turned = block(top, 1, first_count)
+        first = lax.broadcasted_iota(jnp.int32, (16, PART), 1) + top < first_count
+        for i, field, at in each_field():
+            lanes = pl.ds(top, PART)
+            out_ref[0, i, field : field + 16, lanes] = jnp.where(
+                first, out_ref[0, i, field : field + 16, lanes], turned[at : at + 16]
+            )
+
     last = leg_ref[slot, whole:columns, :]
     product = jnp.dot(
         jnp.broadcast_to(last, (16, last.shape[1])), operand[slot], preferred_element_type=jnp.float32

time: 64.9 us -> 64 us (0.986)
  Pallas kernels: 63.1 us -> 62.2 us
    pallas_call x1, Pallas kernels: 56.6 us -> 54.7 us  [fourier_all(): pl.pallas_call(fourier_kernel, grid=(GROUPS,), in_specs=[pl.BlockSpec(mem...]
    pallas_call x1, Pallas kernels: 6.57 us -> 7.51 us  [legendre_all(): pl.pallas_call(legendre_kernel, grid=(slot_count,), in_specs=[pl.BlockSpe...]
where the time goes in v7:
time: 64 us; the launch traced here: 63.8 us
  Pallas kernels  62.2 us (97%)
  local copies, waits for them, and re-layouts  1.61 us (3%)
    pallas_call x1, Pallas kernels, fourier_all(): pl.pallas_call(fourier_kernel, grid=(GROUPS,), in_specs=[pl.BlockSpec(mem...  54.7 us
    pallas_call x1, Pallas kernels, legendre_all(): pl.pallas_call(legendre_kernel, grid=(slot_count,), in_specs=[pl.BlockSpe...  7.51 us

profile of v7, /device:TPU:1, one launch (start us, length us, event | category | flops | bytes accessed | tf_op | source)
XLA Modules:
  0.0 63.8 jit_solution(8214122327993949955)
XLA Ops:
  0.0 0.0 copy-start.1
  0.0 0.9 %reshape.6.order_ref = s32[128,5]{1,0:T(8,128)S(1)} reshape(s32[640]{0:T(1024)} %pair_ref.1) | data formatting | bytes 5120 | tf_op jit(solution)/shard_map/reshape | solution.py:413
  1.0 0.0 copy-start.2
  1.0 0.6 %copy-done.2 = s32[32]{0:T(128)S(1)} copy-done((s32[32]{0:T(128)S(1)}, s32[32]{0:T(128)}, u32[]{:S(2)}) %copy-start.2) | copy-done | bytes 152
  1.6 0.0 copy-start
  1.6 54.7 %fourier.1.operand = bf16[5,512,512]{2,1,0:T(8,128)(2,1)S(1)} custom-call(s32[32]{0:T(128)S(1)} %copy-done.2, s32[128,5]{1,0:T(8,128)S(1)} %reshape.6.order_ref, bf16[4,8,16,5376]{3,2,1,0:T(8,128)(2,1)} %bitcast.3), custom_call_target="tpu_custom_call" | custom-call | tf_op jit(solution)/shard_map/fourier/pallas_call | solution.py:383
  56.3 0.0 copy-done.1
  56.3 0.0 copy-done
  56.3 7.5 %legendre.1 = f32[5,2,64,1281]{3,2,1,0:T(8,128)} custom-call(s32[640]{0:T(1024)S(1)} %copy-done.1, bf16[5,512,512]{2,1,0:T(8,128)(2,1)S(1)} %fourier.1.operand, bf16[5,1281,512]{2,1,0:T(8,128)(2,1)S(1)} %bitcast.2), custom_call_target="tpu_custom_call" | custom-call | tf_op jit(solution)/shard_map/legendre/pallas_call | solution.py:472
Async XLA Ops:
  0.0 56.3 %copy-start.1 = (s32[640]{0:T(1024)S(1)}, s32[640]{0:T(1024)}, u32[]{:S(2)}) copy-start(s32[640]{0:T(1024)} %pair_ref.1) | copy-start | bytes 7684
  1.0 0.7 %copy-start.2 = (s32[32]{0:T(128)S(1)}, s32[32]{0:T(128)}, u32[]{:S(2)}) copy-start(s32[32]{0:T(128)} %length_ref.1) | copy-start | bytes 388
  1.6 54.7 %copy-start = (bf16[5,512,1281]{1,2,0:T(8,128)(2,1)S(1)}, bf16[5,512,1281]{1,2,0:T(8,128)(2,1)}, u32[]{:S(2)}) copy-start(bf16[5,512,1281]{1,2,0:T(8,128)(2,1)} %param.7) | copy-start | bytes 19676164

commit v8 on v6

--- a/solution.py
+++ b/solution.py
@@ -21,7 +21,7 @@
 SPAN = 4
 ORDER = 5
 STRIDE = 13
-PART = 640
+PART = 256
 
 
 def sincos(turns):
@@ -78,9 +78,6 @@
     dest_rows = WAVES * GROUPS // total
     per_dest = WAVES // total
 
-    def place(device):
-        return (device // vert_count, lax.rem(device, vert_count))
-
     @pl.when(g % 2 == 0)
     def _():
         sub = lax.broadcasted_iota(jnp.int32, (8, LANE), 0)
@@ -103,19 +100,28 @@
 
     @pl.when(g == 0)
     def _():
-        for slot in range(2):
-            for q in range(BLOCKS):
-                even[slot, q * 16 : q * 16 + 16, :] = jnp.zeros((16, SUB), jnp.bfloat16)
-            for top in range(0, 3 * BLOCKS * 16, 16):
-                rest[slot, top : top + 16, :] = jnp.zeros((16, 2 * SUB), jnp.bfloat16)
-        barrier = pltpu.get_barrier_semaphore()
+        last = BLOCKS - 1
+        even[1, last * 16 :, LANE:] = jnp.zeros((16, LANE), jnp.bfloat16)
+        for side in range(2):
+            rest[1, last * 48 :, side * SUB + LANE : (side + 1) * SUB] = jnp.zeros((48, LANE), jnp.bfloat16)
+        wa_count = lax.axis_size("wa")
+        wa, vert = lax.axis_index("wa"), lax.axis_index("vert")
+
+        def signal(to_wa, to_vert):
+            pl.semaphore_signal(
+                pltpu.get_barrier_semaphore(), 1, device_id=(to_wa, to_vert), device_id_type=pl.DeviceIdType.MESH
+            )
+
+        for i in range(1, vert_count):
+            signal(wa, lax.rem(vert + i, vert_count))
 
         def greet(i, carry):
-            other = lax.rem(me + i, total)
-            pl.semaphore_signal(barrier, 1, device_id=place(other), device_id_type=pl.DeviceIdType.MESH)
+            to_wa = lax.rem(wa + i, wa_count)
+            for to_vert in range(vert_count):
+                signal(to_wa, to_vert)
             return carry
 
-        lax.fori_loop(1, total, greet, 0)
+        lax.fori_loop(1, wa_count, greet, 0)
         at = lax.broadcasted_iota(jnp.int32, (total, WAVES), 1)
         kind = (at >= CLASS).astype(jnp.int32) + (at >= 2 * CLASS).astype(jnp.int32) + (at >= 3 * CLASS).astype(jnp.int32)
         wave = 4 * (at - CLASS * kind) + kind

time: 64.9 us -> 62.9 us (0.969)
  Pallas kernels: 63.1 us -> 61.1 us
    pallas_call x1, Pallas kernels: 56.6 us -> 54.6 us  [fourier_all(): pl.pallas_call(fourier_kernel, grid=(GROUPS,), in_specs=[pl.BlockSpec(mem...]
where the time goes in v8:
time: 62.9 us; the launch traced here: 62.7 us
  Pallas kernels  61.1 us (97%)
  local copies, waits for them, and re-layouts  1.61 us (3%)
    pallas_call x1, Pallas kernels, fourier_all(): pl.pallas_call(fourier_kernel, grid=(GROUPS,), in_specs=[pl.BlockSpec(mem...  54.6 us
    pallas_call x1, Pallas kernels, legendre_all(): pl.pallas_call(legendre_kernel, grid=(slot_count,), in_specs=[pl.BlockSpe...  6.45 us

profile of v8, /device:TPU:1, one launch (start us, length us, event | category | flops | bytes accessed | tf_op | source)
XLA Modules:
  0.0 62.7 jit_solution(11440984138020189671)
XLA Ops:
  0.0 0.0 copy-start.1
  0.0 0.9 %reshape.6.order_ref = s32[128,5]{1,0:T(8,128)S(1)} reshape(s32[640]{0:T(1024)} %pair_ref.1) | data formatting | bytes 5120 | tf_op jit(solution)/shard_map/reshape | solution.py:413
  1.0 0.0 copy-start.2
  1.0 0.6 %copy-done.2 = s32[32]{0:T(128)S(1)} copy-done((s32[32]{0:T(128)S(1)}, s32[32]{0:T(128)}, u32[]{:S(2)}) %copy-start.2) | copy-done | bytes 152
  1.6 0.0 copy-start
  1.6 54.6 %fourier.1.operand = bf16[5,512,512]{2,1,0:T(8,128)(2,1)S(1)} custom-call(s32[32]{0:T(128)S(1)} %copy-done.2, s32[128,5]{1,0:T(8,128)S(1)} %reshape.6.order_ref, bf16[4,8,16,5376]{3,2,1,0:T(8,128)(2,1)} %bitcast.3), custom_call_target="tpu_custom_call" | custom-call | tf_op jit(solution)/shard_map/fourier/pallas_call | solution.py:383
  56.3 0.0 copy-done.1
  56.3 0.0 copy-done
  56.3 6.5 %legendre.1 = f32[5,2,64,1281]{3,2,1,0:T(8,128)} custom-call(s32[640]{0:T(1024)S(1)} %copy-done.1, bf16[5,512,512]{2,1,0:T(8,128)(2,1)S(1)} %fourier.1.operand, bf16[5,1281,512]{2,1,0:T(8,128)(2,1)S(1)} %bitcast.2), custom_call_target="tpu_custom_call" | custom-call | tf_op jit(solution)/shard_map/legendre/pallas_call | solution.py:463
Async XLA Ops:
  0.0 56.3 %copy-start.1 = (s32[640]{0:T(1024)S(1)}, s32[640]{0:T(1024)}, u32[]{:S(2)}) copy-start(s32[640]{0:T(1024)} %pair_ref.1) | copy-start | bytes 7684
  1.0 0.7 %copy-start.2 = (s32[32]{0:T(128)S(1)}, s32[32]{0:T(128)}, u32[]{:S(2)}) copy-start(s32[32]{0:T(128)} %length_ref.1) | copy-start | bytes 388
  1.6 54.7 %copy-start = (bf16[5,512,1281]{1,2,0:T(8,128)(2,1)S(1)}, bf16[5,512,1281]{1,2,0:T(8,128)(2,1)}, u32[]{:S(2)}) copy-start(bf16[5,512,1281]{1,2,0:T(8,128)(2,1)} %param.7) | copy-start | bytes 19676164

commit v9 on v8

--- a/solution.py
+++ b/solution.py
@@ -349,7 +349,7 @@
                         spread[pl.ds(pl.multiple_of(top, 16), 16), :] = value
                 return carry
 
-            lax.fori_loop(0, half, mirror, 0, unroll=4)
+            lax.fori_loop(0, half, mirror, 0, unroll=8)
             return carry
 
         lax.fori_loop(0, landing.shape[0], arrived, 0)
@@ -371,7 +371,7 @@
                         )
             return carry
 
-        lax.fori_loop(0, half, gather, 0)
+        lax.fori_loop(0, half, gather, 0, unroll=2)
         for tile in range(landing.shape[0]):
             pltpu.make_async_copy(sending.at[tile, others], landing.at[tile, others], send_sem.at[tile]).wait()
 

time: 62.9 us -> 63.1 us (level)
  no operation moved by 1% of the time
where the time goes in v9:
time: 63.1 us; the launch traced here: 63 us
  Pallas kernels  61.3 us (97%)
  local copies, waits for them, and re-layouts  1.61 us (3%)
    pallas_call x1, Pallas kernels, fourier_all(): pl.pallas_call(fourier_kernel, grid=(GROUPS,), in_specs=[pl.BlockSpec(mem...  54.9 us
    pallas_call x1, Pallas kernels, legendre_all(): pl.pallas_call(legendre_kernel, grid=(slot_count,), in_specs=[pl.BlockSpe...  6.45 us

profile of v9, /device:TPU:1, one launch (start us, length us, event | category | flops | bytes accessed | tf_op | source)
XLA Modules:
  0.0 63.0 jit_solution(17492809693667032754)
XLA Ops:
  0.0 0.0 copy-start.1
  0.0 0.9 %reshape.6.order_ref = s32[128,5]{1,0:T(8,128)S(1)} reshape(s32[640]{0:T(1024)} %pair_ref.1) | data formatting | bytes 5120 | tf_op jit(solution)/shard_map/reshape | solution.py:413
  1.0 0.0 copy-start.2
  1.0 0.6 %copy-done.2 = s32[32]{0:T(128)S(1)} copy-done((s32[32]{0:T(128)S(1)}, s32[32]{0:T(128)}, u32[]{:S(2)}) %copy-start.2) | copy-done | bytes 152
  1.6 0.0 copy-start
  1.6 54.9 %fourier.1.operand = bf16[5,512,512]{2,1,0:T(8,128)(2,1)S(1)} custom-call(s32[32]{0:T(128)S(1)} %copy-done.2, s32[128,5]{1,0:T(8,128)S(1)} %reshape.6.order_ref, bf16[4,8,16,5376]{3,2,1,0:T(8,128)(2,1)} %bitcast.3), custom_call_target="tpu_custom_call" | custom-call | tf_op jit(solution)/shard_map/fourier/pallas_call | solution.py:383
  56.5 0.0 copy-done.1
  56.5 0.0 copy-done
  56.5 6.5 %legendre.1 = f32[5,2,64,1281]{3,2,1,0:T(8,128)} custom-call(s32[640]{0:T(1024)S(1)} %copy-done.1, bf16[5,512,512]{2,1,0:T(8,128)(2,1)S(1)} %fourier.1.operand, bf16[5,1281,512]{2,1,0:T(8,128)(2,1)S(1)} %bitcast.2), custom_call_target="tpu_custom_call" | custom-call | tf_op jit(solution)/shard_map/legendre/pallas_call | solution.py:463
Async XLA Ops:
  0.0 56.5 %copy-start.1 = (s32[640]{0:T(1024)S(1)}, s32[640]{0:T(1024)}, u32[]{:S(2)}) copy-start(s32[640]{0:T(1024)} %pair_ref.1) | copy-start | bytes 7684
  1.0 0.7 %copy-start.2 = (s32[32]{0:T(128)S(1)}, s32[32]{0:T(128)}, u32[]{:S(2)}) copy-start(s32[32]{0:T(128)} %length_ref.1) | copy-start | bytes 388
  1.6 54.9 %copy-start = (bf16[5,512,1281]{1,2,0:T(8,128)(2,1)S(1)}, bf16[5,512,1281]{1,2,0:T(8,128)(2,1)}, u32[]{:S(2)}) copy-start(bf16[5,512,1281]{1,2,0:T(8,128)(2,1)} %param.7) | copy-start | bytes 19676164
